TPU v7x, 256 devices: a whole 4x4x8 slice. The times are simulated.
256 devices in a mesh: seq: 4 (over z_lo), hid: 64 (over z_hi, x, y, core).
Axes of the slice: x: 4, y: 4, z: 8 (z_hi: 2, z_lo: 4; z = z_hi * 4 + z_lo), core: 2. Of those that a mesh axis runs over, the one named last changes fastest.
Arguments:
- activations: bfloat16 [512, 8192], P(('seq', 'hid')), may hold values from -6 to 6
- ln_gain: float32 [8192], replicated, may hold values from 0.1 to 1.9
- in_blocks: bfloat16 [2304, 128, 128], P('hid'), may hold values from -0.1875 to 0.1875
- out_blocks: bfloat16 [2304, 128, 128], P('hid'), may hold values from -0.109375 to 0.109375
- block_row: int32 [2304], P('hid'), may hold values from 0 to 63, as said below
- block_col: int32 [2304], P('hid'), may hold values from 0 to 191, as said below
- block_count: int32 [64], P('hid'), may hold values from 12 to 36, as said below
- grad_out: bfloat16 [512, 8192], P(('seq', 'hid')), may hold values from -6 to 6
Outputs:
- layer_out: bfloat16 [512, 8192], P(('seq', 'hid'))
- grad_input: bfloat16 [512, 8192], P(('seq', 'hid'))
- grad_in_blocks: float32 [2304, 128, 128], P('hid')
- grad_out_blocks: float32 [2304, 128, 128], P('hid')
Inputs may be any that keep to these rules, and one draw needn't show every extreme that they name: Slots j * 36 to (j + 1) * 36 - 1 belong to hid index j; within one hid index the slots name distinct pairs of block_row and block_col. `block_col`: slots of hid index j name block columns j * 3 to (j + 1) * 3 - 1. Slot s belongs to hid index j = s // 36 and is live when s - j * 36 < block_count[j]: the live slots of hid index j are its first block_count[j]; some hid index has all 36 live.
All inputs are finite; a program needn't handle non-finite values.
Results may differ from a plain program's by a relative error of at most 0.0053.
Values may be sent and summed in bfloat16 or wider, within the bound.
A program may use at most 128 MiB of HBM per device.

v0:
```python
import jax
import jax.numpy as jnp
from jax import lax
from jax.sharding import PartitionSpec as P

FF = 24576


def normalize(activations, ln_gain):
    values = activations.astype(jnp.float32)
    row_mean = jnp.mean(values, axis=-1, keepdims=True)
    centered = values - row_mean
    variance = jnp.mean(centered * centered, axis=-1, keepdims=True)
    inv_std = lax.rsqrt(variance + 1e-05)
    x_hat = centered * inv_std
    return (x_hat, inv_std, (x_hat * ln_gain).astype(jnp.bfloat16))


def local(activations, ln_gain, in_blocks, out_blocks, block_row, block_col, block_count, grad_out):
    high = lax.Precision.HIGHEST
    x_hat, inv_std, normed = normalize(activations, ln_gain)
    normed_all = lax.all_gather(normed, "hid", axis=0, tiled=True)
    grads_all = lax.all_gather(grad_out, "hid", axis=0, tiled=True)
    width = activations.shape[1]
    slot_count = in_blocks.shape[0]
    block_size = in_blocks.shape[1]
    row_blocks = width // block_size
    local_cols = FF // block_size // lax.axis_size("hid")
    hidden_width = local_cols * block_size
    live_mask = (jnp.arange(slot_count, dtype=jnp.int32) < block_count[0]).astype(jnp.float32)
    local_col = block_col - lax.axis_index("hid") * local_cols
    places = jax.nn.one_hot(
        block_row * local_cols + local_col, row_blocks * local_cols, dtype=jnp.float32
    )
    places = places * live_mask[:, None]
    grid_in = jnp.einsum(
        "sp,sij->pij", places.astype(jnp.bfloat16), in_blocks, preferred_element_type=jnp.float32
    )
    grid_out = jnp.einsum(
        "sp,sij->pij", places.astype(jnp.bfloat16), out_blocks, preferred_element_type=jnp.float32
    )
    grid_in = grid_in.astype(jnp.bfloat16).reshape(row_blocks, local_cols, block_size, block_size)
    grid_out = grid_out.astype(jnp.bfloat16).reshape(row_blocks, local_cols, block_size, block_size)
    dense_in = grid_in.transpose(0, 2, 1, 3).reshape(width, hidden_width)
    dense_out = grid_out.transpose(1, 2, 0, 3).reshape(hidden_width, width)
    pre = jnp.dot(normed_all, dense_in, preferred_element_type=jnp.float32)
    hidden = jax.nn.silu(pre).astype(jnp.bfloat16)
    grad_hidden = lax.dot_general(
        grads_all, dense_out, (((1,), (1,)), ((), ())), preferred_element_type=jnp.float32
    )
    sig = jax.nn.sigmoid(pre)
    grad_pre = (grad_hidden * sig * (1.0 + pre * (1.0 - sig))).astype(jnp.bfloat16)
    whole_in = lax.dot_general(
        normed_all, grad_pre, (((0,), (0,)), ((), ())), preferred_element_type=jnp.float32
    )
    whole_out = lax.dot_general(
        hidden, grads_all, (((0,), (0,)), ((), ())), preferred_element_type=jnp.float32
    )
    whole_in = whole_in.reshape(row_blocks, block_size, local_cols, block_size).transpose(
        0, 2, 1, 3
    )
    whole_out = whole_out.reshape(local_cols, block_size, row_blocks, block_size).transpose(
        2, 0, 1, 3
    )
    whole_in = whole_in.reshape(row_blocks * local_cols, block_size, block_size)
    whole_out = whole_out.reshape(row_blocks * local_cols, block_size, block_size)
    grad_first = jnp.einsum("sp,pij->sij", places, whole_in, precision=high)
    grad_second = jnp.einsum("sp,pij->sij", places, whole_out, precision=high)
    rows_here = hidden
    out_sum = lax.psum_scatter(
        jnp.dot(rows_here, dense_out, preferred_element_type=jnp.float32),
        "hid",
        scatter_dimension=0,
        tiled=True,
    )
    rows_here = grad_pre
    grad_normed = lax.psum_scatter(
        lax.dot_general(
            rows_here, dense_in, (((1,), (1,)), ((), ())), preferred_element_type=jnp.float32
        ),
        "hid",
        scatter_dimension=0,
        tiled=True,
    )
    grad_first, grad_second = lax.psum((grad_first, grad_second), "seq")
    layer_out = (activations.astype(jnp.float32) + out_sum).astype(jnp.bfloat16)
    scaled = grad_normed * ln_gain
    mean_g = jnp.mean(scaled, axis=-1, keepdims=True)
    mean_gx = jnp.mean(scaled * x_hat, axis=-1, keepdims=True)
    grad_input = (
        inv_std * (scaled - mean_g - x_hat * mean_gx) + grad_out.astype(jnp.float32)
    ).astype(jnp.bfloat16)
    return (layer_out, grad_input, grad_first, grad_second)


def solution(mesh):
    in_specs = (
        P(("seq", "hid"), None),
        P(),
        P("hid", None, None),
        P("hid", None, None),
        P("hid"),
        P("hid"),
        P("hid"),
        P(("seq", "hid"), None),
    )
    out_specs = (
        P(("seq", "hid"), None),
        P(("seq", "hid"), None),
        P("hid", None, None),
        P("hid", None, None),
    )
    return jax.shard_map(local, mesh=mesh, in_specs=in_specs, out_specs=out_specs, check_vma=False)
```

profile of v0, /device:TPU:1, one launch (start us, length us, event | category | flops | bytes accessed | tf_op | source)
XLA Modules:
  0.0 1317.8 jit_solution(14684669417360925771)
XLA Ops:
  7.2 0.0 copy-start
  7.2 0.0 all-gather.5.cloned.1.call-start
  7.2 1.0 convert_reduce_fusion
  8.3 1.0 fusion.32
  9.3 1.5 fusion.34
  10.8 0.0 all-gather.5.cloned.1.call-update
  10.8 0.0 all-gather.7.cloned.1.call-start
  10.9 0.7 all-gather.7.cloned.1.call-update
  11.6 0.0 all-reduce.9.cloned.1.call-start
  12.3 0.7 subtract_add_fusion
  12.9 0.0 copy-done
  13.0 1.9 convolution_convert_fusion.1
  14.9 6.7 copy.34
  21.6 0.0 copy-start.4
  21.6 9.4 copy.35
  30.9 0.0 copy-done.4
  30.9 1.9 convolution_convert_fusion
  32.9 4.0 copy.37
  36.9 6.7 copy.38
  43.6 55.6 %all-gather.5.cloned.1.call-done = bf16[64,2,8192]{2,1,0:T(2,128)(2,1)} async-done(((bf16[1,2,8192]{2,1,0:T(2,128)(2,1)}), bf16[64,2,8192]{2,1,0:T(2,128)(2,1)}) %all-gather.5.cloned.1.call-update) | async-done | bytes 2097168 | tf_op jit(solution)/shard_map/all_gather | solution.py:22
  99.2 2.7 reshape.68
  102.0 6.8 fusion.10
  108.8 70.9 %all-gather.7.cloned.1.call-done = bf16[64,2,8192]{2,1,0:T(2,128)(2,1)} async-done(((bf16[1,2,8192]{2,1,0:T(2,128)(2,1)}), bf16[64,2,8192]{2,1,0:T(2,128)(2,1)}) %all-gather.7.cloned.1.call-update) | async-done | bytes 2097168 | tf_op jit(solution)/shard_map/all_gather | solution.py:23
  179.7 4.5 reshape.70
  184.2 0.0 copy-start.2
  184.2 8.2 convolution_bitcast_fusion
  192.4 0.0 copy-done.2
  192.4 6.8 fusion.27
  199.2 11.8 copy.52
  211.0 16.6 %copy.43 = f32[3,128,64,128]{3,1,0,2:T(8,128)} copy(f32[3,128,64,128]{3,2,1,0:T(8,128)} %bitcast.74) | data formatting | bytes 25165824 | tf_op jit(solution)/shard_map/reshape | solution.py:62
  227.6 20.8 %fusion = f32[36,128,128]{2,0,1:T(8,128)} fusion(f32[192,128,128]{2,1,0:T(8,128)} %bitcast.77, f32[36]{0:T(128)S(1)} %compare_convert_fusion, s32[36]{0:T(128)S(1)} %subtract_add_fusion), kind=kOutput, calls=%fused_computation | convolution fusion | flops 1358968320 | bytes 14942496 | tf_op jit(solution)/shard_map/sp,pij->sij/dot_general | solution.py:68
  248.4 6.3 convolution_bitcast_fusion.1
  254.7 11.9 copy.51
  266.7 12.6 copy.41
  279.3 20.6 %fusion.2 = f32[36,128,128]{2,0,1:T(8,128)} fusion(f32[192,128,128]{2,1,0:T(8,128)} %bitcast.76, f32[36]{0:T(128)S(1)} %compare_convert_fusion, s32[36]{0:T(128)S(1)} %subtract_add_fusion), kind=kOutput, calls=%fused_computation.2 | convolution fusion | flops 1358968320 | bytes 14942496 | tf_op jit(solution)/shard_map/sp,pij->sij/dot_general | solution.py:67
  299.9 0.0 all-reduce.9.cloned.1.call-update
  299.9 0.3 all-reduce.7.cloned.1.call-start
  300.2 8.9 fusion.8
  309.2 8.9 fusion.6
  318.1 0.0 copy-start.8
  318.1 0.0 all-reduce.7.cloned.1.call-update
  318.1 0.6 copy-done.8
  318.8 0.6 dynamic-slice
  320.0 172.7 %all-reduce.9.cloned.1.call-done = (f32[36,128,128]{2,0,1:T(8,128)}, f32[36,128,128]{2,0,1:T(8,128)}) async-done(((f32[36,128,128]{2,0,1:T(8,128)}, f32[36,128,128]{2,0,1:T(8,128)}), (f32[36,128,128]{2,0,1:T(8,128)}, f32[36,128,128]{2,0,1:T(8,128)})) %all-reduce.9.cloned.1.call-update) | async-done | bytes 4718608 | tf_op jit(solution)/shard_map/psum | solution.py:85
  492.7 0.0 copy-start.3
  492.7 0.0 copy-start.1
  492.7 0.0 copy-start.5
  492.7 0.0 copy-start.6
  492.7 0.0 copy-start.7
  492.7 3.8 copy.45
  496.5 0.0 copy-done.3
  496.5 1.8 copy.46
  498.3 809.4 %all-reduce.7.cloned.1.call-done = (f32[128,8192]{1,0:T(8,128)}, f32[128,8192]{1,0:T(8,128)}) async-done(((f32[128,8192]{1,0:T(8,128)}, f32[128,8192]{1,0:T(8,128)}), (f32[128,8192]{1,0:T(8,128)}, f32[128,8192]{1,0:T(8,128)})) %all-reduce.7.cloned.1.call-update) | async-done | bytes 8388624
  1307.7 0.0 copy-done.5
  1307.7 0.0 copy-done.6
  1307.7 1.2 fusion.54
  1309.0 0.0 copy-done.7
  1309.0 1.8 add_convert_fusion
  1310.8 0.0 copy-done.1
  (4 shorter events, 0.0 us)
Async XLA Ops:
  7.2 5.8 copy-start
  7.2 92.0 %all-gather.5.cloned.1.call-start = ((), (), s32[]{:S(2)}) async-start(), calls=%async_computation | async-start | bytes 2129920 | tf_op jit(solution)/shard_map/all_gather | solution.py:22
  10.8 168.9 %all-gather.7.cloned.1.call-start = ((), (), s32[]{:S(2)}) async-start(), calls=%async_computation.1 | async-start | bytes 2129920 | tf_op jit(solution)/shard_map/all_gather | solution.py:23
  11.6 481.1 %all-reduce.9.cloned.1.call-start = ((), (), s32[]{:S(2)}) async-start(), calls=%async_computation.3 | async-start | bytes 10485760 | tf_op jit(solution)/shard_map/psum | solution.py:85
  21.6 9.4 copy-start.4
  184.2 8.2 copy-start.2
  299.9 1007.8 %all-reduce.7.cloned.1.call-start = ((), (), s32[]{:S(2)}) async-start(), calls=%async_computation.2 | async-start | bytes 16777216
  318.1 0.7 copy-start.8
  492.7 3.8 copy-start.3
  492.7 818.1 %copy-start.1 = (bf16[36,128,128]{2,1,0:T(8,128)(2,1)S(1)}, bf16[36,128,128]{2,1,0:T(8,128)(2,1)}, u32[]{:S(2)}) copy-start(bf16[36,128,128]{2,1,0:T(8,128)(2,1)} %param.10) | copy-start | bytes 3538948
  492.7 815.0 %copy-start.5 = (bf16[2,8192]{1,0:T(2,128)(2,1)S(1)}, bf16[2,8192]{1,0:T(2,128)(2,1)}, u32[]{:S(2)}) copy-start(bf16[2,8192]{1,0:T(2,128)(2,1)} %param.8) | copy-start | bytes 98308
  492.7 815.0 %copy-start.6 = (f32[8192]{0:T(1024)S(1)}, f32[8192]{0:T(1024)}, u32[]{:S(2)}) copy-start(f32[8192]{0:T(1024)} %param.9) | copy-start | bytes 98308
  492.7 816.3 %copy-start.7 = (bf16[2,8192]{1,0:T(2,128)(2,1)S(1)}, bf16[2,8192]{1,0:T(2,128)(2,1)}, u32[]{:S(2)}) copy-start(bf16[2,8192]{1,0:T(2,128)(2,1)} %param.15) | copy-start | bytes 98308
Sparse Core Ops, SparseCore 0:
  12.2 87.0 all-gather.4
  102.8 76.8 all-gather.6
  300.1 192.5 all-reduce.8
  495.2 812.4 all-reduce.6
where the time goes:
time: 1320 us
  waiting for transfers between devices  1110 us (84%)
  local copies, waits for them, and re-layouts  93.9 us (7%)
  matrix products  91.2 us (7%)
  between operations  15.6 us (1%)
    unnamed x5, waiting for transfers between devices  810 us
    psum x1, waiting for transfers between devices, local(): grad_first, grad_second = lax.psum((grad_first, grad_second), 'seq')  173 us
    all_gather x1, waiting for transfers between devices, local(): grads_all = lax.all_gather(grad_out, 'hid', axis=0, tiled=True)  70.9 us
    all_gather x1, waiting for transfers between devices, local(): normed_all = lax.all_gather(normed, 'hid', axis=0, tiled=True)  55.6 us
    unnamed x25, local copies, waits for them, and re-layouts  37.8 us
  transfers between devices with their start and end apart: 4, of which 4 were waited for; matrix products, arithmetic and copies ran while one was open for 5% of the time, Pallas kernels for 0%

commit v1 on v0

v1 whole, which is shorter than its diff:
```python
import functools

import jax
import jax.numpy as jnp
from jax import lax
from jax.experimental import pallas as pl
from jax.experimental.pallas import tpu as pltpu
from jax.sharding import PartitionSpec as P

F32 = jnp.float32
BF16 = jnp.bfloat16
MESH = pl.DeviceIdType.MESH
WIDTH = 8192
SLOTS = 36
COLS = 3
CHUNK = 2
CHUNKS = 2 * SLOTS // CHUNK
LAG = 4


def place():
    seq, hid = lax.axis_index("seq"), lax.axis_index("hid")
    return seq, hid // 32, (hid // 8) % 4, (hid // 2) % 4, hid % 2


def device(seq, zh, x, y, core):
    return (seq, zh * 32 + x * 8 + y * 2 + core)


def remote(src, dst, send, recv, to):
    return pltpu.make_async_remote_copy(
        src_ref=src, dst_ref=dst, send_sem=send, recv_sem=recv, device_id=to, device_id_type=MESH
    )


def meet(peers):
    barrier = pltpu.get_barrier_semaphore()
    for peer in peers:
        pl.semaphore_signal(barrier, inc=1, device_id=peer, device_id_type=MESH)
    pl.semaphore_wait(barrier, len(peers))


def octet_peers(seq, zh, x, y, core):
    offsets = [(dx, dc) for dx in (2, 1, 3, 0) for dc in (0, 1) if (dx, dc) != (0, 0)]
    return [((x + dx) % 4, (core + dc) % 2) for dx, dc in offsets]


def layer_norm(act_ref):
    values = act_ref[...].astype(F32)
    mean = jnp.sum(values, axis=-1, keepdims=True) * (1.0 / WIDTH)
    centered = values - mean
    variance = jnp.sum(centered * centered, axis=-1, keepdims=True) * (1.0 / WIDTH)
    inv_std = lax.rsqrt(variance + 1e-05)
    return centered * inv_std, inv_std


def gather_kernel(
    act_ref, gain_ref, grad_ref, all_ref,
    wide, packed, landed,
    a2a_send, a2a_recv, zh_send, zh_recv, s1_send, s1_recv, s2_send, s2_recv, sw_send, sw_recv,
):
    seq, zh, x, y, core = place()
    me = x * 2 + core
    octet = octet_peers(seq, zh, x, y, core)
    xs = [(x + d) % 4 for d in (1, 2, 3)]
    ys = [(y + d) % 4 for d in (1, 2, 3)]
    partner = device(seq, 1 - zh, x, y, core)
    sibling = device(seq, zh, x, y, 1 - core)
    meet(
        [device(seq, zh, px, y, pc) for px, pc in octet]
        + [device(seq, zh, x, py, core) for py in ys]
        + [partner]
    )
    x_hat, _ = layer_norm(act_ref)
    for a, rows in enumerate((x_hat * gain_ref[...], grad_ref[...].astype(F32))):
        for p in range(64):
            wide[a, 2 * p : 2 * p + 2, :] = rows[:, p * 128 : (p + 1) * 128]
        packed[a] = wide[a].astype(BF16).reshape(8, 16, 128)
    copies = []
    for k, (px, pc) in enumerate(octet):
        copies.append(
            remote(
                packed.at[:, px * 2 + pc], landed.at[:, me], a2a_send.at[k], a2a_recv.at[k],
                device(seq, zh, px, y, pc),
            )
        )
        copies[-1].start()
    landed[:, me] = packed[:, me]
    for copy in copies:
        copy.wait_recv()
    for a in range(2):
        wide[a] = landed[a].astype(F32).reshape(128, 128)
        for p in range(8):
            first = wide[a, pl.ds(2 * p, 8, stride=16), :]
            second = wide[a, pl.ds(2 * p + 1, 8, stride=16), :]
            all_ref[a, x, core, p, zh, y] = jnp.concatenate([first, second], axis=0).astype(BF16)
    own = all_ref.at[:, x, core, :, zh, y]
    cross = remote(own, own, zh_send, zh_recv, partner)
    cross.start()

    def stage_one(plane, zp):
        out = []
        for d in range(3):
            block = all_ref.at[0, x, core, :, zp, y]
            out.append(
                remote(block, block, s1_send.at[plane, 0, d], s1_recv.at[plane, 0, d],
                       device(seq, zh, xs[d], y, core))
            )
            block = all_ref.at[1, x, core, :, zp, y]
            out.append(
                remote(block, block, s1_send.at[plane, 1, d], s1_recv.at[plane, 1, d],
                       device(seq, zh, x, ys[d], core))
            )
        for copy in out:
            copy.start()
        return out

    def stage_two(plane, zp):
        out = []
        for d in range(3):
            block = all_ref.at[0, :, core, :, zp, y]
            out.append(
                remote(block, block, s2_send.at[plane, 0, d], s2_recv.at[plane, 0, d],
                       device(seq, zh, x, ys[d], core))
            )
            block = all_ref.at[1, x, core, :, zp]
            out.append(
                remote(block, block, s2_send.at[plane, 1, d], s2_recv.at[plane, 1, d],
                       device(seq, zh, xs[d], y, core))
            )
        for copy in out:
            copy.start()
        return out

    def swap(plane, zp):
        out = []
        for a in range(2):
            block = all_ref.at[a, :, core, :, zp]
            out.append(remote(block, block, sw_send.at[plane, a], sw_recv.at[plane, a], sibling))
        for copy in out:
            copy.start()
        return out

    def landed_all(group):
        for copy in group:
            copy.wait_recv()

    one = stage_one(0, zh)
    landed_all(one)
    two = stage_two(0, zh)
    cross.wait_recv()
    one_far = stage_one(1, 1 - zh)
    landed_all(one_far)
    two_far = stage_two(1, 1 - zh)
    landed_all(two)
    sw = swap(0, zh)
    landed_all(two_far)
    sw_far = swap(1, 1 - zh)
    landed_all(sw)
    landed_all(sw_far)
    for copy in copies + [cross] + one + two + one_far + two_far + sw + sw_far:
        copy.wait_send()


def gather(act, gain, grad):
    vmem = pl.BlockSpec(memory_space=pltpu.VMEM)
    dma = pltpu.SemaphoreType.DMA
    return pl.pallas_call(
        gather_kernel,
        out_shape=jax.ShapeDtypeStruct((2, 4, 2, 8, 2, 4, 16, 128), BF16),
        in_specs=[vmem] * 3,
        out_specs=vmem,
        scratch_shapes=[
            pltpu.VMEM((2, 128, 128), F32),
            pltpu.VMEM((2, 8, 16, 128), BF16),
            pltpu.VMEM((2, 8, 16, 128), BF16),
            dma((7,)), dma((7,)), dma, dma,
            dma((2, 2, 3)), dma((2, 2, 3)), dma((2, 2, 3)), dma((2, 2, 3)),
            dma((2, 2)), dma((2, 2)),
        ],
        compiler_params=pltpu.CompilerParams(
            collective_id=1, has_side_effects=True, vmem_limit_bytes=32 << 20
        ),
        name="gather_rows",
    )(act, gain, grad)


def dot(a, b, dims):
    return lax.dot_general(a, b, (dims, ((), ())), preferred_element_type=F32)


GROUP = 4


def compute_kernel(
    row_ref, col_ref, count_ref, all_ref, in_ref, out_ref, sums_ref, grads_ref,
    pre, grad_hidden, hidden, grad_pre, total,
):
    first_col = lax.axis_index("hid") * COLS
    count = count_ref[0]
    pre[...] = jnp.zeros_like(pre)
    grad_hidden[...] = jnp.zeros_like(grad_hidden)

    def up(g, _):
        parts = []
        for k in range(GROUP):
            s = g * GROUP + k
            row = row_ref[s]
            live = s < count
            one = dot(all_ref[0, row], in_ref[s], ((1,), (0,)))
            two = dot(all_ref[1, row], out_ref[s], ((1,), (1,)))
            parts.append((s, jnp.where(live, one, 0.0), jnp.where(live, two, 0.0)))
        for s, one, two in parts:
            col = col_ref[s] - first_col
            pre[col] += one
            grad_hidden[col] += two
        return 0

    lax.fori_loop(0, SLOTS // GROUP, up, 0)
    for c in range(COLS):
        value = pre[c]
        sig = jax.nn.sigmoid(value)
        hidden[c] = (value * sig).astype(BF16)
        grad_pre[c] = (grad_hidden[c] * sig * (1.0 + value * (1.0 - sig))).astype(BF16)

    def clear(p, _):
        total[0, p] = jnp.zeros((128, 128), F32)
        total[1, p] = jnp.zeros((128, 128), F32)
        return 0

    lax.fori_loop(0, 64, clear, 0)

    def down(g, _):
        parts = []
        for k in range(GROUP):
            s = g * GROUP + k
            row = row_ref[s]
            col = col_ref[s] - first_col
            live = s < count
            h, gp = hidden[col], grad_pre[col]
            one = dot(h, out_ref[s], ((1,), (0,)))
            two = dot(gp, in_ref[s], ((1,), (1,)))
            three = dot(all_ref[0, row], gp, ((0,), (0,)))
            four = dot(h, all_ref[1, row], ((0,), (0,)))
            parts.append((s, row, jnp.where(live, one, 0.0), jnp.where(live, two, 0.0)))
            grads_ref[s] = jnp.where(live, three, 0.0).astype(BF16)
            grads_ref[s + SLOTS] = jnp.where(live, four, 0.0).astype(BF16)
        for s, row, one, two in parts:
            total[0, row] += one
            total[1, row] += two
        return 0

    lax.fori_loop(0, SLOTS // GROUP, down, 0)

    def narrow(p, _):
        sums_ref[0, p] = total[0, p].astype(BF16)
        sums_ref[1, p] = total[1, p].astype(BF16)
        return 0

    lax.fori_loop(0, 64, narrow, 0)


def compute(rows, cols, count, everything, in_blocks, out_blocks):
    vmem = pl.BlockSpec(memory_space=pltpu.VMEM)
    smem = pl.BlockSpec(memory_space=pltpu.SMEM)
    return pl.pallas_call(
        compute_kernel,
        out_shape=(
            jax.ShapeDtypeStruct((2, 64, 128, 128), BF16),
            jax.ShapeDtypeStruct((2 * SLOTS, 128, 128), BF16),
        ),
        in_specs=[smem] * 3 + [vmem] * 3,
        out_specs=(vmem, vmem),
        scratch_shapes=[
            pltpu.VMEM((COLS, 128, 128), F32),
            pltpu.VMEM((COLS, 128, 128), F32),
            pltpu.VMEM((COLS, 128, 128), BF16),
            pltpu.VMEM((COLS, 128, 128), BF16),
            pltpu.VMEM((2, 64, 128, 128), F32),
        ],
        compiler_params=pltpu.CompilerParams(vmem_limit_bytes=40 << 20),
        name="block_products",
    )(rows, cols, count, everything, in_blocks, out_blocks)


def reduce_kernel(
    act_ref, gain_ref, grad_ref, sums_ref, part_ref, out_ref, gin_ref, total_ref,
    swap_a, swap_b, half_a, half_b, near_a, near_b, quart_a, quart_b, far_a, far_b,
    keep, cross_src, cross_dst, wide, back, rows,
    end_in, mid_own, mid_in,
    sw_send, sw_recv, n_send, n_recv, f_send, f_recv, zh_send, zh_recv, b_send, b_recv,
    e_send, e_recv, m_send, m_recv, t_send, t_recv,
):
    seq, zh, x, y, core = place()
    me = x * 2 + core
    octet = octet_peers(seq, zh, x, y, core)
    partner = device(seq, 1 - zh, x, y, core)
    sibling = device(seq, zh, x, y, 1 - core)
    beside = device(seq + 1 - 2 * (seq % 2), zh, x, y, core)
    across = device(3 - seq, zh, x, y, core)
    is_mid = jnp.logical_or(seq == 1, seq == 2)
    is_end = jnp.logical_or(seq == 0, seq == 3)
    meet(
        [device(seq, zh, px, y, pc) for px, pc in octet]
        + [device(seq, zh, x, (y + d) % 4, core) for d in (1, 2, 3)]
        + [partner, beside, across]
    )

    def chunk(ref, k):
        return ref.at[pl.ds(k * CHUNK, CHUNK)]

    def end_copy(k):
        return remote(chunk(part_ref, k), chunk(end_in, k), e_send.at[k], e_recv.at[k], beside)

    def mid_copy(k):
        return remote(chunk(mid_own, k), chunk(mid_in, k), m_send.at[k], m_recv.at[k], across)

    def total_copy(k):
        return remote(chunk(total_ref, k), chunk(total_ref, k), t_send.at[k], t_recv.at[k], beside)

    def mid_first(k):
        end_copy(k).wait_recv()
        for j in range(CHUNK):
            s = k * CHUNK + j
            mid_own[s] = (end_in[s].astype(F32) + part_ref[s].astype(F32)).astype(BF16)
        mid_copy(k).start()

    def mid_second(k):
        mid_copy(k).wait_recv()
        for j in range(CHUNK):
            s = k * CHUNK + j
            total_ref[s] = (mid_own[s].astype(F32) + mid_in[s].astype(F32)).astype(BF16)
        total_copy(k).start()

    done = [0]

    def chain(steps):
        start, stop = done[0], min(done[0] + steps, CHUNKS + LAG)
        done[0] = stop

        @pl.when(is_mid)
        def _():
            def step(k, _):
                @pl.when(k < CHUNKS)
                def _():
                    mid_first(k)

                @pl.when(k >= LAG)
                def _():
                    mid_second(k - LAG)

                return 0

            lax.fori_loop(start, stop, step, 0)

    order = (2, 1, 3, 0)
    swaps = []
    for d in order:
        pair = (
            remote(sums_ref.at[0, (x + d) % 4, 1 - core], swap_a.at[d],
                   sw_send.at[0, d], sw_recv.at[0, d], sibling),
            remote(sums_ref.at[1, :, 1 - core, :, :, (y + d) % 4], swap_b.at[d],
                   sw_send.at[1, d], sw_recv.at[1, d], sibling),
        )
        for copy in pair:
            copy.start()
        swaps.append(pair)

    @pl.when(is_end)
    def _():
        def step(k, _):
            end_copy(k).start()
            return 0

        lax.fori_loop(0, CHUNKS, step, 0)

    nears = []
    for d, (copy_a, copy_b) in zip(order[:3], swaps):
        copy_a.wait_recv()

        def add_a(p, _):
            half_a[d, p] = (
                sums_ref[0, (x + d) % 4, core, p].astype(F32) + swap_a[d, p].astype(F32)
            ).astype(BF16)
            return 0

        lax.fori_loop(0, 8, add_a, 0)
        nears.append(
            remote(half_a.at[d], near_a.at[d], n_send.at[0, d], n_recv.at[0, d],
                   device(seq, zh, (x + d) % 4, y, core))
        )
        nears[-1].start()
        copy_b.wait_recv()

        def add_b(p, _):
            for v in range(4):
                half_b[d, v, p] = (
                    sums_ref[1, v, core, p, :, (y + d) % 4].astype(F32)
                    + swap_b[d, v, p].astype(F32)
                ).astype(BF16)
            return 0

        lax.fori_loop(0, 8, add_b, 0)
        nears.append(
            remote(half_b.at[d], near_b.at[d], n_send.at[1, d], n_recv.at[1, d],
                   device(seq, zh, x, (y + d) % 4, core))
        )
        nears[-1].start()
        chain(1)
    for copy in swaps[3]:
        copy.wait_recv()
    chain(6)
    for copy in nears:
        copy.wait_recv()

    def sum_a(p, _):
        value = sums_ref[0, x, core, p].astype(F32) + swap_a[0, p].astype(F32)
        for d in (1, 2, 3):
            value += near_a[d, p].astype(F32)
        quart_a[p] = value.astype(BF16)
        return 0

    lax.fori_loop(0, 8, sum_a, 0)
    fars = []
    for d in order[:3]:
        fars.append(
            remote(quart_a.at[:, :, (y + d) % 4], far_a.at[d], f_send.at[0, d], f_recv.at[0, d],
                   device(seq, zh, x, (y + d) % 4, core))
        )
        fars[-1].start()

    def sum_b(p, _):
        for v in range(4):
            value = sums_ref[1, v, core, p, :, y].astype(F32) + swap_b[0, v, p].astype(F32)
            for d in (1, 2, 3):
                value += near_b[d, v, p].astype(F32)
            quart_b[v, p] = value.astype(BF16)
        return 0

    lax.fori_loop(0, 8, sum_b, 0)
    for d in order[:3]:
        fars.append(
            remote(quart_b.at[(x + d) % 4], far_b.at[d], f_send.at[1, d], f_recv.at[1, d],
                   device(seq, zh, (x + d) % 4, y, core))
        )
        fars[-1].start()
    chain(3)
    for copy in fars:
        copy.wait_recv()

    def sum_far(p, _):
        one = quart_a[p, :, y].astype(F32)
        two = quart_b[x, p].astype(F32)
        for d in (1, 2, 3):
            one += far_a[d, p].astype(F32)
            two += far_b[d, p].astype(F32)
        keep[0, p] = one
        keep[1, p] = two
        cross_src[0, :, p] = one.astype(BF16)
        cross_src[1, :, p] = two.astype(BF16)
        return 0

    lax.fori_loop(0, 8, sum_far, 0)
    cross = remote(cross_src.at[:, 1 - zh], cross_dst, zh_send, zh_recv, partner)
    cross.start()
    chain(3)
    cross.wait_recv()
    for a in range(2):
        for p in range(8):
            value = keep[a, p, zh] + cross_dst[a, p].astype(F32)
            wide[a, pl.ds(2 * p, 8, stride=16), :] = value[0:8]
            wide[a, pl.ds(2 * p + 1, 8, stride=16), :] = value[8:16]
    for a in range(2):
        back[a] = wide[a].reshape(8, 16, 128)
    backs = []
    for k, (px, pc) in enumerate(octet):
        backs.append(
            remote(back.at[:, px * 2 + pc], rows.at[:, me], b_send.at[k], b_recv.at[k],
                   device(seq, zh, px, y, pc))
        )
        backs[-1].start()
    rows[:, me] = back[:, me]
    chain(2)
    for copy in backs:
        copy.wait_recv()
    sums = []
    for a in range(2):
        sums.append(
            jnp.concatenate(
                [rows[a, p // 8, 2 * (p % 8) : 2 * (p % 8) + 2, :] for p in range(64)], axis=1
            )
        )
    x_hat, inv_std = layer_norm(act_ref)
    out_ref[...] = (act_ref[...].astype(F32) + sums[0]).astype(BF16)
    scaled = sums[1] * gain_ref[...]
    mean_g = jnp.sum(scaled, axis=-1, keepdims=True) * (1.0 / WIDTH)
    mean_gx = jnp.sum(scaled * x_hat, axis=-1, keepdims=True) * (1.0 / WIDTH)
    gin_ref[...] = (
        inv_std * (scaled - mean_g - x_hat * mean_gx) + grad_ref[...].astype(F32)
    ).astype(BF16)
    chain(CHUNKS + LAG)

    @pl.when(is_mid)
    def _():
        def step(k, _):
            mid_copy(k).wait_send()
            total_copy(k).wait_send()
            return 0

        lax.fori_loop(0, CHUNKS, step, 0)

    @pl.when(is_end)
    def _():
        def step(k, _):
            end_copy(k).wait_send()
            total_copy(k).wait_recv()
            return 0

        lax.fori_loop(0, CHUNKS, step, 0)

    for pair in swaps:
        for copy in pair:
            copy.wait_send()
    for copy in nears + fars + [cross] + backs:
        copy.wait_send()


def reduce(act, gain, grad, sums, parts):
    vmem = pl.BlockSpec(memory_space=pltpu.VMEM)
    dma = pltpu.SemaphoreType.DMA
    slot = (2 * SLOTS, 128, 128)
    return pl.pallas_call(
        reduce_kernel,
        out_shape=(
            jax.ShapeDtypeStruct((2, WIDTH), BF16),
            jax.ShapeDtypeStruct((2, WIDTH), BF16),
            jax.ShapeDtypeStruct(slot, BF16),
        ),
        in_specs=[vmem] * 5,
        out_specs=(vmem, vmem, vmem),
        scratch_shapes=[
            pltpu.VMEM((4, 8, 2, 4, 16, 128), BF16),
            pltpu.VMEM((4, 4, 8, 2, 16, 128), BF16),
            pltpu.VMEM((4, 8, 2, 4, 16, 128), BF16),
            pltpu.VMEM((4, 4, 8, 2, 16, 128), BF16),
            pltpu.VMEM((4, 8, 2, 4, 16, 128), BF16),
            pltpu.VMEM((4, 4, 8, 2, 16, 128), BF16),
            pltpu.VMEM((8, 2, 4, 16, 128), BF16),
            pltpu.VMEM((4, 8, 2, 16, 128), BF16),
            pltpu.VMEM((4, 8, 2, 16, 128), BF16),
            pltpu.VMEM((4, 8, 2, 16, 128), BF16),
            pltpu.VMEM((2, 8, 2, 16, 128), F32),
            pltpu.VMEM((2, 2, 8, 16, 128), BF16),
            pltpu.VMEM((2, 8, 16, 128), BF16),
            pltpu.VMEM((2, 128, 128), F32),
            pltpu.VMEM((2, 8, 16, 128), F32),
            pltpu.VMEM((2, 8, 16, 128), F32),
            pltpu.VMEM(slot, BF16),
            pltpu.VMEM(slot, BF16),
            pltpu.VMEM(slot, BF16),
            dma((2, 4)), dma((2, 4)), dma((2, 4)), dma((2, 4)), dma((2, 4)), dma((2, 4)),
            dma, dma, dma((7,)), dma((7,)),
            dma((CHUNKS,)), dma((CHUNKS,)), dma((CHUNKS,)), dma((CHUNKS,)),
            dma((CHUNKS,)), dma((CHUNKS,)),
        ],
        compiler_params=pltpu.CompilerParams(
            collective_id=2, has_side_effects=True, vmem_limit_bytes=48 << 20
        ),
        name="reduce_sums",
    )(act, gain, grad, sums, parts)


def local(activations, ln_gain, in_blocks, out_blocks, block_row, block_col, block_count, grad_out):
    gain = ln_gain.reshape(1, WIDTH)
    everything = gather(activations, gain, grad_out)
    sums, parts = compute(
        block_row, block_col, block_count, everything.reshape(2, 64, 128, 128), in_blocks, out_blocks
    )
    layer_out, grad_input, totals = reduce(
        activations, gain, grad_out, sums.reshape(2, 4, 2, 8, 2, 4, 16, 128), parts
    )
    return (
        layer_out, grad_input, totals[:SLOTS].astype(F32), totals[SLOTS:].astype(F32),
    )


def solution(mesh):
    rows, blocks, slots = P(("seq", "hid"), None), P("hid", None, None), P("hid")
    in_specs = (rows, P(), blocks, blocks, slots, slots, slots, rows)
    out_specs = (rows, rows, blocks, blocks)
    return jax.shard_map(local, mesh=mesh, in_specs=in_specs, out_specs=out_specs, check_vma=False)
```

time: 1320 us -> 131 us (0.10)
  waiting for transfers between devices: 1110 us -> 0 us
  Pallas kernels: 0 us -> 121 us
  matrix products: 91.2 us -> 0 us
  local copies, waits for them, and re-layouts: 93.9 us -> 5.47 us
  between operations: 15.6 us -> 1.55 us
    unnamed x5 -> x0, waiting for transfers between devices: 810 us -> none
    psum x1 -> x0, waiting for transfers between devices: 173 us -> none  [local(): grad_first, grad_second = lax.psum((grad_first, grad_second), 'seq')]
    all_gather x2 -> x0, waiting for transfers between devices: 126 us -> none  [the longest x1 70.9 us: local(): grads_all = lax.all_gather(grad_out, 'hid', axis=0, tiled=True)]
    pallas_call x0 -> x3, Pallas kernels: none -> 121 us  [the longest x1 74.3 us: reduce(): pl.pallas_call(reduce_kernel, out_shape=(jax.ShapeDtypeStruct((2, WIDTH),...]
    dot_general x10 -> x0, matrix products: 91.2 us -> none  [the longest x1 20.8 us: local(): grad_second = jnp.einsum('sp,pij->sij', places, whole_out, precision=high)]
    unnamed x25 -> x24, local copies, waits for them, and re-layouts: 37.8 us -> 5.47 us
    transpose x3 -> x0, local copies, waits for them, and re-layouts: 28.7 us -> none  [the longest x1 12.6 us: local(): whole_in.reshape(row_blocks, block_size, local_cols, block_size)]
    reshape x1 -> x0, local copies, waits for them, and re-layouts: 16.6 us -> none  [local(): whole_out.reshape(local_cols, block_size, row_blocks, block_size)]
  transfers between devices with their start and end apart: 4 -> 0, of which waited for: 4 -> 0; matrix products, arithmetic and copies ran while one was open for 5% -> 0% of each run, Pallas kernels for 0% -> 0%
where the time goes in v1:
time: 131 us
  Pallas kernels  121 us (92%)
  local copies, waits for them, and re-layouts  5.47 us (4%)
  other arithmetic  2.79 us (2%)
  between operations  1.55 us (1%)
    pallas_call x1, Pallas kernels, reduce(): pl.pallas_call(reduce_kernel, out_shape=(jax.ShapeDtypeStruct((2, WIDTH),...  74.3 us
    pallas_call x1, Pallas kernels, gather(): pl.pallas_call(gather_kernel, out_shape=jax.ShapeDtypeStruct((2, 4, 2, 8,...  39.3 us
    pallas_call x1, Pallas kernels, compute(): pl.pallas_call(compute_kernel, out_shape=(jax.ShapeDtypeStruct((2, 64, 12...  7.51 us
    unnamed x24, local copies, waits for them, and re-layouts  5.47 us
    convert_element_type x1, other arithmetic, local(): totals[SLOTS:].astype(F32)  2.79 us

profile of v1, /device:TPU:1, one launch (start us, length us, event | category | flops | bytes accessed | tf_op | source)
XLA Modules:
  0.0 131.0 jit_solution(774251297008707796)
XLA Ops:
  0.6 0.0 copy-start.2
  0.6 0.0 copy-start.1
  1.4 0.0 copy-start.3
  1.5 0.7 copy-done.3
  2.2 0.0 copy-start.5
  2.2 0.8 copy-done.5
  3.0 0.0 copy-start.7
  3.0 0.8 copy-done.7
  3.7 0.0 copy-start.9
  3.7 0.0 copy-start.10
  3.7 39.3 %gather_rows.1 = bf16[2,4,2,8,2,4,16,128]{7,6,5,4,3,2,1,0:T(8,128)(2,1)S(1)} custom-call(bf16[2,8192]{1,0:T(2,128)(2,1)S(1)} %copy-done.3, f32[1,8192]{1,0:T(1,128)S(1)} %bitcast.5, bf16[2,8192]{1,0:T(2,128)(2,1)S(1)} %copy-done.7), custom_call_target="tpu_custom_call" | custom-call | tf_op jit(solution)/shard_map/gather_rows/pallas_call | solution.py:168
  43.1 0.0 copy-done.2
  43.1 0.0 copy-done.1
  43.1 0.0 copy-done.9
  43.1 0.0 copy-done.10
  43.1 0.0 copy-start.4
  43.1 0.0 copy-start.6
  43.1 0.0 copy-start.8
  43.2 7.5 %block_products.1 = (bf16[2,64,128,128]{3,2,1,0:T(8,128)(2,1)S(1)}, bf16[72,128,128]{2,1,0:T(8,128)(2,1)S(1)}) custom-call(s32[36]{0:T(128)S(1)} %copy-done.9, s32[36]{0:T(128)S(1)} %copy-done.10, s32[1]{0:T(128)S(6)} %copy.14.count_ref, bf16[2,64,128,128]{3,2,1,0:T(8,128)(2,1)S(1)} %bitcast.3, bf16[36,128,128]{2,1,0:T(8,128)(2,1)S(1)} %copy-done.1, ...), custom_call_target="tpu_custom_call" | custom-call | tf_op jit(solution)/shard_map/block_products/pallas_call | solution.py:266
  50.7 0.0 copy-start
  50.7 1.9 %copy-done = bf16[2,64,128,128]{3,2,1,0:T(8,128)(2,1)} copy-done((bf16[2,64,128,128]{3,2,1,0:T(8,128)(2,1)}, bf16[2,64,128,128]{3,2,1,0:T(8,128)(2,1)S(1)}, u32[]{:S(2)}) %copy-start) | copy-done | bytes 4194328
  52.6 0.0 copy-done.4
  52.6 0.0 copy-done.6
  52.6 0.0 copy-done.8
  52.6 74.3 %reduce_sums.1 = (bf16[2,8192]{1,0:T(2,128)(2,1)S(1)}, bf16[2,8192]{1,0:T(2,128)(2,1)S(1)}, bf16[72,128,128]{2,1,0:T(8,128)(2,1)S(1)}) custom-call(bf16[2,8192]{1,0:T(2,128)(2,1)S(1)} %copy-done.4, f32[1,8192]{1,0:T(1,128)S(1)} %bitcast.6, bf16[2,8192]{1,0:T(2,128)(2,1)S(1)} %copy-done.8, bf16[2,4,2,8,2,4,16,128]{7,6,5,4,3,2,1,0:T(8,128)(2,1)} %bitcast.4, ...), custom_call_target="tpu_custom_call" | custom-call | tf_op jit(solution)/shard_map/reduce_sums/pallas_call | solution.py:532
  126.9 2.8 %slice_convert_fusion = (f32[36,128,128]{2,1,0:T(8,128)}, f32[36,128,128]{2,1,0:T(8,128)}) fusion(bf16[72,128,128]{2,1,0:T(8,128)(2,1)S(1)} %get-tuple-element.13), kind=kLoop, calls=%fused_computation | loop fusion | flops 1179648 | bytes 7077888 | tf_op jit(solution)/shard_map/convert_element_type | solution.py:583
  129.7 0.6 copy.15
  130.4 0.6 copy.16
Async XLA Ops:
  0.6 42.5 %copy-start.2 = (bf16[36,128,128]{2,1,0:T(8,128)(2,1)S(1)}, bf16[36,128,128]{2,1,0:T(8,128)(2,1)}, u32[]{:S(2)}) copy-start(bf16[36,128,128]{2,1,0:T(8,128)(2,1)} %out_ref.1) | copy-start | bytes 3538948
  0.6 42.5 %copy-start.1 = (bf16[36,128,128]{2,1,0:T(8,128)(2,1)S(1)}, bf16[36,128,128]{2,1,0:T(8,128)(2,1)}, u32[]{:S(2)}) copy-start(bf16[36,128,128]{2,1,0:T(8,128)(2,1)} %in_ref.1) | copy-start | bytes 3538948
  1.4 0.8 copy-start.3
  2.2 0.8 copy-start.5
  3.0 0.8 copy-start.7
  3.7 39.4 %copy-start.9 = (s32[36]{0:T(128)S(1)}, s32[36]{0:T(128)}, u32[]{:S(2)}) copy-start(s32[36]{0:T(128)} %row_ref.1) | copy-start | bytes 436
  3.7 39.4 %copy-start.10 = (s32[36]{0:T(128)S(1)}, s32[36]{0:T(128)}, u32[]{:S(2)}) copy-start(s32[36]{0:T(128)} %col_ref.1) | copy-start | bytes 436
  43.1 9.5 %copy-start.4 = (bf16[2,8192]{1,0:T(2,128)(2,1)S(1)}, bf16[2,8192]{1,0:T(2,128)(2,1)}, u32[]{:S(2)}) copy-start(bf16[2,8192]{1,0:T(2,128)(2,1)} %act_ref.3) | copy-start | bytes 98308
  43.1 9.5 %copy-start.6 = (f32[8192]{0:T(1024)S(1)}, f32[8192]{0:T(1024)}, u32[]{:S(2)}) copy-start(f32[8192]{0:T(1024)} %param.9) | copy-start | bytes 98308
  43.1 9.5 %copy-start.8 = (bf16[2,8192]{1,0:T(2,128)(2,1)S(1)}, bf16[2,8192]{1,0:T(2,128)(2,1)}, u32[]{:S(2)}) copy-start(bf16[2,8192]{1,0:T(2,128)(2,1)} %grad_ref.3) | copy-start | bytes 98308
  50.7 1.9 %copy-start = (bf16[2,64,128,128]{3,2,1,0:T(8,128)(2,1)}, bf16[2,64,128,128]{3,2,1,0:T(8,128)(2,1)S(1)}, u32[]{:S(2)}) copy-start(bf16[2,64,128,128]{3,2,1,0:T(8,128)(2,1)S(1)} %get-tuple-element.9) | copy-start | bytes 12582916

commit v2 on v1

v2 whole, which is shorter than its diff:
```python
import functools

import jax
import jax.numpy as jnp
from jax import lax
from jax.experimental import pallas as pl
from jax.experimental.pallas import tpu as pltpu
from jax.sharding import PartitionSpec as P

F32 = jnp.float32
BF16 = jnp.bfloat16
MESH = pl.DeviceIdType.MESH
WIDTH = 8192
SLOTS = 36
COLS = 3
CHUNK = 1
CHUNKS = SLOTS // CHUNK
LAG = 5


def place():
    seq, hid = lax.axis_index("seq"), lax.axis_index("hid")
    return seq, hid // 32, (hid // 8) % 4, (hid // 2) % 4, hid % 2


def device(seq, zh, x, y, core):
    return (seq, zh * 32 + x * 8 + y * 2 + core)


def remote(src, dst, send, recv, to):
    return pltpu.make_async_remote_copy(
        src_ref=src, dst_ref=dst, send_sem=send, recv_sem=recv, device_id=to, device_id_type=MESH
    )


def meet(peers):
    barrier = pltpu.get_barrier_semaphore()
    for peer in peers:
        pl.semaphore_signal(barrier, inc=1, device_id=peer, device_id_type=MESH)
    pl.semaphore_wait(barrier, len(peers))


def octet_peers(seq, zh, x, y, core):
    offsets = [(dx, dc) for dx in (2, 1, 3, 0) for dc in (0, 1) if (dx, dc) != (0, 0)]
    return [((x + dx) % 4, (core + dc) % 2) for dx, dc in offsets]


def layer_norm(act_ref):
    values = act_ref[...].astype(F32)
    mean = jnp.sum(values, axis=-1, keepdims=True) * (1.0 / WIDTH)
    centered = values - mean
    variance = jnp.sum(centered * centered, axis=-1, keepdims=True) * (1.0 / WIDTH)
    inv_std = lax.rsqrt(variance + 1e-05)
    return centered * inv_std, inv_std


def gather_kernel(
    act_hbm, gain_hbm, grad_hbm, all_ref, outer_y, outer_x,
    act_ref, gain_ref, grad_ref, wide, packed, landed,
    local_sem, a2a_send, a2a_recv, z_send, z_recv, s1_send, s1_recv,
    s2_send, s2_recv, fw_send, fw_recv, sw_send, sw_recv, o_send, o_recv,
):
    seq, zh, x, y, core = place()
    me = x * 2 + core
    octet = octet_peers(seq, zh, x, y, core)
    xs = [(x + d) % 4 for d in (1, 3, 2)]
    ys = [(y + d) % 4 for d in (1, 3, 2)]
    planes = (zh, 1 - zh)
    sibling = device(seq, zh, x, y, 1 - core)
    loads = [
        pltpu.make_async_copy(src, dst, local_sem.at[k])
        for k, (src, dst) in enumerate(
            ((act_hbm, act_ref), (gain_hbm, gain_ref), (grad_hbm, grad_ref))
        )
    ]
    for load in loads:
        load.start()
    targets = [(0, px, pc) for px, pc in octet] + [(1, px, pc) for px, pc in octet]
    targets.append((1, x, core))
    peers = [device(seq, planes[f], px, y, pc) for f, px, pc in targets]
    peers += [device(seq, zh, x, py, core) for py in ys]
    peers += [device((seq + d) % 4, zh, x, y, core) for d in (1, 2, 3)]
    barrier = pltpu.get_barrier_semaphore()
    for peer in peers:
        pl.semaphore_signal(barrier, inc=1, device_id=peer, device_id_type=MESH)
    for load in loads:
        load.wait()
    x_hat, _ = layer_norm(act_ref)
    for a, rows in enumerate((x_hat * gain_ref[...], grad_ref[...].astype(F32))):
        for p in range(64):
            wide[a, 2 * p : 2 * p + 2, :] = rows[:, p * 128 : (p + 1) * 128]
        packed[a] = wide[a].astype(BF16).reshape(8, 16, 128)
    pl.semaphore_wait(barrier, len(peers))
    near, far = [], []
    for k, (f, px, pc) in enumerate(targets):
        copy = remote(
            packed.at[:, px * 2 + pc], landed.at[zh, :, me], a2a_send.at[k], a2a_recv.at[k],
            peers[k],
        )
        copy.start()
        (far if f else near).append(copy)
    landed[zh, :, me] = packed[:, me]

    def relayout(zp):
        for a in range(2):
            wide[a] = landed[zp, a].astype(F32).reshape(128, 128)
            for p in range(8):
                first = wide[a, pl.ds(2 * p, 8, stride=16), :]
                second = wide[a, pl.ds(2 * p + 1, 8, stride=16), :]
                all_ref[a, x, core, p, zp, y] = jnp.concatenate([first, second], axis=0).astype(BF16)

    stage_ones, stage_twos, forwards, swaps, lines, outers = {}, {}, {}, [], [], []

    def stage_one(f):
        zp = planes[f]
        for a in (0, 1):
            block = all_ref.at[a, x, core, :, zp, y]
            out = []
            for d in range(3):
                to = device(seq, zh, xs[d], y, core) if a == 0 else device(seq, zh, x, ys[d], core)
                out.append(remote(block, block, s1_send.at[f, a, d], s1_recv.at[f, a, d], to))
                out[-1].start()
            stage_ones[f, a] = out

    def piece(f, other, nx, ny):
        return outer_x.at[other, nx] if f else outer_y.at[other, :, ny]

    def along_z(f):
        zp = planes[f]
        for d in (1, 2, 3):
            lines.append(
                remote(all_ref.at[1, x, core, :, zp, y], piece(f, seq, x, y),
                       z_send.at[f, d - 1], z_recv.at[f, d - 1],
                       device((seq + d) % 4, zh, x, y, core))
            )
            lines[-1].start()

    def outer_first():
        for f in range(2):
            for k in range(3):
                lines[3 * f + 2 - k].wait_recv()
                block = piece(f, (seq + k + 1) % 4, x, y)
                for d in range(3):
                    to = device(seq, zh, xs[d], y, core) if f else device(seq, zh, x, ys[d], core)
                    outers.append(
                        remote(block, block, o_send.at[f, k, d], o_recv.at[f, k, d], to)
                    )
                    outers[-1].start()

    def part(f, a, nx, ny, half):
        zp = planes[f]
        if a == 0:
            if half is None:
                return all_ref.at[0, :, core, :, zp, ny]
            return all_ref.at[0, pl.ds(2 * half, 2), core, :, zp, ny]
        if half is None:
            return all_ref.at[1, nx, core, :, zp]
        return all_ref.at[1, nx, core, pl.ds(4 * half, 4), zp]

    def ahead(a, d):
        if a == 0:
            return device(seq, zh, x, ys[d], core)
        return device(seq, zh, xs[d], y, core)

    def swap(f, a, k, block):
        copy = remote(block, block, sw_send.at[f, a, k], sw_recv.at[f, a, k], sibling)
        copy.start()
        swaps.append(copy)

    def stage_two(f):
        for a in (0, 1):
            for copy in stage_ones[f, a]:
                copy.wait_recv()
            block = part(f, a, x, y, None)
            out = []
            for d in range(2):
                out.append(
                    remote(block, block, s2_send.at[f, a, d], s2_recv.at[f, a, d], ahead(a, d))
                )
                out[-1].start()
            stage_twos[f, a] = out
        for a in (0, 1):
            swap(f, a, 0, part(f, a, x, y, None))

    def forward(f):
        for a in (0, 1):
            out = []
            for d in range(2):
                stage_twos[f, a][d].wait_recv()
                block = part(f, a, xs[1 - d], ys[1 - d], d)
                out.append(
                    remote(block, block, fw_send.at[f, a, d], fw_recv.at[f, a, d], ahead(a, d))
                )
                out[-1].start()
            forwards[f, a] = out
            for d in range(2):
                swap(f, a, 1 + d, part(f, a, xs[1 - d], ys[1 - d], None))

    def finish(f):
        for a in (0, 1):
            for copy in forwards[f, a]:
                copy.wait_recv()
            swap(f, a, 3, part(f, a, xs[2], ys[2], None))

    for copy in near:
        copy.wait_recv()
    relayout(zh)
    stage_one(0)
    for copy in far:
        copy.wait_recv()
    relayout(1 - zh)
    stage_one(1)
    stage_two(0)
    along_z(0)
    along_z(1)
    stage_two(1)
    forward(0)
    forward(1)
    outer_first()
    finish(0)
    finish(1)
    for copy in swaps + outers:
        copy.wait_recv()
    for copy in near + far + lines + swaps + outers:
        copy.wait_send()
    for group in (stage_ones, stage_twos, forwards):
        for copies in group.values():
            for copy in copies:
                copy.wait_send()


def gather(act, gain, grad):
    vmem = pl.BlockSpec(memory_space=pltpu.VMEM)
    hbm = pl.BlockSpec(memory_space=pltpu.HBM)
    dma = pltpu.SemaphoreType.DMA
    return pl.pallas_call(
        gather_kernel,
        out_shape=(
            jax.ShapeDtypeStruct((2, 4, 2, 8, 2, 4, 16, 128), BF16),
            jax.ShapeDtypeStruct((4, 8, 4, 16, 128), BF16),
            jax.ShapeDtypeStruct((4, 4, 8, 16, 128), BF16),
        ),
        in_specs=[hbm] * 3,
        out_specs=(vmem, vmem, vmem),
        scratch_shapes=[
            pltpu.VMEM((2, WIDTH), BF16),
            pltpu.VMEM((1, WIDTH), F32),
            pltpu.VMEM((2, WIDTH), BF16),
            pltpu.VMEM((2, 128, 128), F32),
            pltpu.VMEM((2, 8, 16, 128), BF16),
            pltpu.VMEM((2, 2, 8, 16, 128), BF16),
            dma((3,)), dma((15,)), dma((15,)), dma((2, 3)), dma((2, 3)),
            dma((2, 2, 3)), dma((2, 2, 3)), dma((2, 2, 2)), dma((2, 2, 2)),
            dma((2, 2, 2)), dma((2, 2, 2)), dma((2, 2, 4)), dma((2, 2, 4)),
            dma((2, 3, 3)), dma((2, 3, 3)),
        ],
        compiler_params=pltpu.CompilerParams(
            collective_id=1, has_side_effects=True, vmem_limit_bytes=12 << 20
        ),
        cost_estimate=pl.CostEstimate(flops=0, bytes_accessed=64 << 20, transcendentals=0),
        name="gather_rows",
    )(*(pltpu.with_memory_space_constraint(v, pltpu.HBM) for v in (act, gain, grad)))


def dot(a, b, dims):
    return lax.dot_general(a, b, (dims, ((), ())), preferred_element_type=F32)


GROUP = 4


def compute_kernel(
    row_hbm, col_hbm, count_ref, all_ref, in_hbm, out_hbm, sums_ref, grads_ref, hidden,
    row_ref, col_ref, in_ref, out_ref, pre, grad_hidden, grad_pre, total, local_sem,
):
    first_col = lax.axis_index("hid") * COLS
    loads = [
        pltpu.make_async_copy(src, dst, local_sem.at[k])
        for k, (src, dst) in enumerate(
            ((row_hbm, row_ref), (col_hbm, col_ref), (in_hbm, in_ref), (out_hbm, out_ref))
        )
    ]
    for load in loads:
        load.start()

    def clear(p, _):
        total[0, p] = jnp.zeros((128, 128), F32)
        total[1, p] = jnp.zeros((128, 128), F32)
        return 0

    lax.fori_loop(0, 64, clear, 0)
    pre[...] = jnp.zeros_like(pre)
    grad_hidden[...] = jnp.zeros_like(grad_hidden)
    for load in loads:
        load.wait()
    count = count_ref[0]

    def up(g, _):
        parts = []
        for k in range(GROUP):
            s = g * GROUP + k
            row = row_ref[s]
            live = s < count
            one = dot(all_ref[0, row], in_ref[s], ((1,), (0,)))
            two = dot(all_ref[1, row], out_ref[s], ((1,), (1,)))
            parts.append((s, jnp.where(live, one, 0.0), jnp.where(live, two, 0.0)))
        for s, one, two in parts:
            col = col_ref[s] - first_col
            pre[col] += one
            grad_hidden[col] += two
        return 0

    lax.fori_loop(0, SLOTS // GROUP, up, 0)
    for c in range(COLS):
        value = pre[c]
        sig = jax.nn.sigmoid(value)
        hidden[c] = (value * sig).astype(BF16)
        grad_pre[c] = (grad_hidden[c] * sig * (1.0 + value * (1.0 - sig))).astype(BF16)

    def down(g, _):
        parts = []
        for k in range(GROUP):
            s = g * GROUP + k
            row = row_ref[s]
            col = col_ref[s] - first_col
            live = s < count
            h, gp = hidden[col], grad_pre[col]
            one = dot(h, out_ref[s], ((1,), (0,)))
            two = dot(gp, in_ref[s], ((1,), (1,)))
            three = dot(all_ref[0, row], gp, ((0,), (0,)))
            parts.append((s, row, jnp.where(live, one, 0.0), jnp.where(live, two, 0.0)))
            grads_ref[s] = jnp.where(live, three, 0.0).astype(BF16)
        for s, row, one, two in parts:
            total[0, row] += one
            total[1, row] += two
        return 0

    lax.fori_loop(0, SLOTS // GROUP, down, 0)

    def narrow(p, _):
        sums_ref[0, p] = total[0, p].astype(BF16)
        sums_ref[1, p] = total[1, p].astype(BF16)
        return 0

    lax.fori_loop(0, 64, narrow, 0)


def compute(rows, cols, count, everything, in_blocks, out_blocks):
    vmem = pl.BlockSpec(memory_space=pltpu.VMEM)
    hbm = pl.BlockSpec(memory_space=pltpu.HBM)
    pin = functools.partial(pltpu.with_memory_space_constraint, memory_space=pltpu.HBM)
    return pl.pallas_call(
        compute_kernel,
        out_shape=(
            jax.ShapeDtypeStruct((2, 64, 128, 128), BF16),
            jax.ShapeDtypeStruct((SLOTS, 128, 128), BF16),
            jax.ShapeDtypeStruct((COLS, 128, 128), BF16),
        ),
        in_specs=[hbm] * 2 + [pl.BlockSpec(memory_space=pltpu.SMEM)] + [vmem] + [hbm] * 2,
        out_specs=(vmem, vmem, vmem),
        scratch_shapes=[
            pltpu.SMEM((SLOTS,), jnp.int32),
            pltpu.SMEM((SLOTS,), jnp.int32),
            pltpu.VMEM((SLOTS, 128, 128), BF16),
            pltpu.VMEM((SLOTS, 128, 128), BF16),
            pltpu.VMEM((COLS, 128, 128), F32),
            pltpu.VMEM((COLS, 128, 128), F32),
            pltpu.VMEM((COLS, 128, 128), BF16),
            pltpu.VMEM((2, 64, 128, 128), F32),
            pltpu.SemaphoreType.DMA((4,)),
        ],
        compiler_params=pltpu.CompilerParams(vmem_limit_bytes=24 << 20),
        name="block_products",
    )(pin(rows), pin(cols), count, everything, pin(in_blocks), pin(out_blocks))


def reduce_kernel(
    sums_ref, part_ref, hidden_ref, all_ref, outer_y, outer_x,
    rows, total_ref, hiddens_ref, grads_ref,
    swap_a, swap_b, half_a, half_b, near_a, near_b, quart_a, quart_b, far_a, far_b,
    wide, back,
    end_in, mid_own, mid_in,
    sw_send, sw_recv, n_send, n_recv, f_send, f_recv, b_send, b_recv,
    e_send, e_recv, m_send, m_recv, t_send, t_recv,
    h_send, h_recv, own_sem, ob_send, ob_recv, of_send, of_recv, os_send, os_recv,
):
    seq, zh, x, y, core = place()
    me = x * 2 + core
    octet = octet_peers(seq, zh, x, y, core)
    sibling = device(seq, zh, x, y, 1 - core)
    beside = device(seq + 1 - 2 * (seq % 2), zh, x, y, core)
    across = device(3 - seq, zh, x, y, core)
    is_mid = jnp.logical_or(seq == 1, seq == 2)
    is_end = jnp.logical_or(seq == 0, seq == 3)
    targets = [(zh, px, pc) for px, pc in octet] + [(1 - zh, px, pc) for px, pc in octet]
    targets.append((1 - zh, x, core))
    meet(
        [device(seq, zt, px, y, pc) for zt, px, pc in targets]
        + [device(seq, zh, x, (y + d) % 4, core) for d in (1, 2, 3)]
        + [device((seq + d) % 4, zh, x, y, core) for d in (1, 2, 3)]
    )
    others = [(seq + d) % 4 for d in (1, 2, 3)]
    xs = [(x + d) % 4 for d in (1, 3, 2)]
    ys = [(y + d) % 4 for d in (1, 3, 2)]

    def chunk(ref, k):
        return ref.at[pl.ds(k * CHUNK, CHUNK)]

    def end_copy(k):
        return remote(chunk(part_ref, k), chunk(end_in, k), e_send.at[k], e_recv.at[k], beside)

    def mid_copy(k):
        return remote(chunk(mid_own, k), chunk(mid_in, k), m_send.at[k], m_recv.at[k], across)

    def total_copy(k):
        return remote(chunk(total_ref, k), chunk(total_ref, k), t_send.at[k], t_recv.at[k], beside)

    def mid_first(k):
        end_copy(k).wait_recv()
        for j in range(CHUNK):
            s = k * CHUNK + j
            mid_own[s] = (end_in[s].astype(F32) + part_ref[s].astype(F32)).astype(BF16)
        mid_copy(k).start()

    def mid_second(k):
        mid_copy(k).wait_recv()
        for j in range(CHUNK):
            s = k * CHUNK + j
            total_ref[s] = (mid_own[s].astype(F32) + mid_in[s].astype(F32)).astype(BF16)
        total_copy(k).start()

    done = [0]

    def chain(steps):
        start, stop = done[0], min(done[0] + steps, CHUNKS + LAG)
        done[0] = stop

        @pl.when(is_mid)
        def _():
            def step(k, _):
                @pl.when(k < CHUNKS)
                def _():
                    mid_first(k)

                @pl.when(k >= LAG)
                def _():
                    mid_second(k - LAG)

                return 0

            lax.fori_loop(start, stop, step, 0)

    order = (2, 1, 3, 0)
    swaps = []
    for d in order:
        pair = (
            remote(sums_ref.at[0, (x + d) % 4, 1 - core], swap_a.at[d],
                   sw_send.at[0, d], sw_recv.at[0, d], sibling),
            remote(sums_ref.at[1, :, 1 - core, :, :, (y + d) % 4], swap_b.at[d],
                   sw_send.at[1, d], sw_recv.at[1, d], sibling),
        )
        for copy in pair:
            copy.start()
        swaps.append(pair)

    own_rows = pltpu.make_async_copy(all_ref.at[1], grads_ref.at[seq], own_sem)
    own_rows.start()
    hiddens_ref[seq] = hidden_ref[...]
    near_end = seq + 1 - 2 * (seq % 2)
    mid = 3 - seq
    far_end = mid + 1 - 2 * (mid % 2)

    def hidden_copy(source, k, to):
        block = hiddens_ref.at[source]
        return remote(block, block, h_send.at[k], h_recv.at[source], to)

    outer_b, outer_f, outer_s = [], [], []
    planes = (zh, 1 - zh)
    for other in others:
        for n in range(8):
            grads_ref[other, x, core, n, zh] = outer_y[other, n]
        for n in range(4):
            grads_ref[other, n, core, :, 1 - zh, y] = outer_x[other, n]

    def outer_block(other, f, nx, ny, half):
        if f:
            if half is None:
                return grads_ref.at[other, :, core, :, planes[1], ny]
            return grads_ref.at[other, pl.ds(2 * half, 2), core, :, planes[1], ny]
        if half is None:
            return grads_ref.at[other, nx, core, :, planes[0]]
        return grads_ref.at[other, nx, core, pl.ds(4 * half, 4), planes[0]]

    def outer_to(f, d):
        return device(seq, zh, x, ys[d], core) if f else device(seq, zh, xs[d], y, core)

    def outer_swap(k, f, n, block):
        copy = remote(block, block, os_send.at[k, f, n], os_recv.at[k, f, n], sibling)
        copy.start()
        outer_s.append(copy)

    def outer_second(k):
        other = others[k]
        for f in range(2):
            block = outer_block(other, f, x, y, None)
            for d in range(2):
                outer_b.append(
                    remote(block, block, ob_send.at[k, f, d], ob_recv.at[k, f, d], outer_to(f, d))
                )
                outer_b[-1].start()
        for f in range(2):
            outer_swap(k, f, 0, outer_block(other, f, x, y, None))

    def outer_forward(k):
        other = others[k]
        for f in range(2):
            for d in range(2):
                outer_b[4 * k + 2 * f + d].wait_recv()
                block = outer_block(other, f, xs[1 - d], ys[1 - d], d)
                outer_f.append(
                    remote(block, block, of_send.at[k, f, d], of_recv.at[k, f, d], outer_to(f, d))
                )
                outer_f[-1].start()
            for d in range(2):
                outer_swap(k, f, 1 + d, outer_block(other, f, xs[1 - d], ys[1 - d], None))

    def outer_finish(k):
        other = others[k]
        for f in range(2):
            for d in range(2):
                outer_f[4 * k + 2 * f + d].wait_recv()
            outer_swap(k, f, 3, outer_block(other, f, xs[2], ys[2], None))

    @pl.when(is_end)
    def _():
        def step(k, _):
            end_copy(k).start()
            return 0

        lax.fori_loop(0, 12, step, 0)
        hidden_copy(seq, 0, beside).start()
        lax.fori_loop(12, CHUNKS, step, 0)

    @pl.when(is_mid)
    def _():
        hidden_copy(seq, 0, beside).start()
        hidden_copy(seq, 1, across).start()

    outer_second(0)
    nears = []
    for d, (copy_a, copy_b) in zip(order[:3], swaps):
        copy_a.wait_recv()

        def add_a(p, _):
            half_a[d, p] = (
                sums_ref[0, (x + d) % 4, core, p].astype(F32) + swap_a[d, p].astype(F32)
            ).astype(BF16)
            return 0

        lax.fori_loop(0, 8, add_a, 0)
        nears.append(
            remote(half_a.at[d], near_a.at[d], n_send.at[0, d], n_recv.at[0, d],
                   device(seq, zh, (x + d) % 4, y, core))
        )
        nears[-1].start()
        copy_b.wait_recv()

        def add_b(p, _):
            for v in range(4):
                half_b[d, v, p] = (
                    sums_ref[1, v, core, p, :, (y + d) % 4].astype(F32)
                    + swap_b[d, v, p].astype(F32)
                ).astype(BF16)
            return 0

        lax.fori_loop(0, 8, add_b, 0)
        nears.append(
            remote(half_b.at[d], near_b.at[d], n_send.at[1, d], n_recv.at[1, d],
                   device(seq, zh, x, (y + d) % 4, core))
        )
        nears[-1].start()
        chain(2)
    for copy in swaps[3]:
        copy.wait_recv()
    for copy in nears:
        chain(3)
        copy.wait_recv()

    @pl.when(is_mid)
    def _():
        hidden_copy(near_end, 0, beside).wait_recv()
        hidden_copy(near_end, 2, across).start()
        hidden_copy(mid, 0, beside).wait_recv()
        hidden_copy(mid, 3, beside).start()


    def sum_a(p, _):
        value = sums_ref[0, x, core, p].astype(F32) + swap_a[0, p].astype(F32)
        for d in (1, 2, 3):
            value += near_a[d, p].astype(F32)
        quart_a[p] = value.astype(BF16)
        return 0

    lax.fori_loop(0, 8, sum_a, 0)
    fars = []
    for d in order[:3]:
        fars.append(
            remote(quart_a.at[:, :, (y + d) % 4], far_a.at[d], f_send.at[0, d], f_recv.at[0, d],
                   device(seq, zh, x, (y + d) % 4, core))
        )
        fars[-1].start()

    def sum_b(p, _):
        for v in range(4):
            value = sums_ref[1, v, core, p, :, y].astype(F32) + swap_b[0, v, p].astype(F32)
            for d in (1, 2, 3):
                value += near_b[d, v, p].astype(F32)
            quart_b[v, p] = value.astype(BF16)
        return 0

    lax.fori_loop(0, 8, sum_b, 0)
    for d in order[:3]:
        fars.append(
            remote(quart_b.at[(x + d) % 4], far_b.at[d], f_send.at[1, d], f_recv.at[1, d],
                   device(seq, zh, (x + d) % 4, y, core))
        )
        fars[-1].start()
    outer_second(1)
    outer_second(2)
    for copy in fars:
        chain(1)
        copy.wait_recv()

    def sum_far(p, _):
        one = quart_a[p, :, y].astype(F32)
        two = quart_b[x, p].astype(F32)
        for d in (1, 2, 3):
            one += far_a[d, p].astype(F32)
            two += far_b[d, p].astype(F32)
        for zt in range(2):
            for a, value in enumerate((one[zt], two[zt])):
                wide[zt, a, pl.ds(2 * p, 8, stride=16), :] = value[0:8]
                wide[zt, a, pl.ds(2 * p + 1, 8, stride=16), :] = value[8:16]
        return 0

    lax.fori_loop(0, 8, sum_far, 0)
    for zt in range(2):
        for a in range(2):
            back[zt, a] = wide[zt, a].astype(BF16).reshape(8, 16, 128)
    backs = []
    for k, (zt, px, pc) in enumerate(targets):
        backs.append(
            remote(back.at[zt, :, px * 2 + pc], rows.at[zh, :, me], b_send.at[k], b_recv.at[k],
                   device(seq, zt, px, y, pc))
        )
        backs[-1].start()
    rows[zh, :, me] = back[zh, :, me]
    outer_forward(0)
    chain(5)

    @pl.when(is_mid)
    def _():
        hidden_copy(far_end, 0, beside).wait_recv()
        hidden_copy(far_end, 4, beside).start()

    outer_forward(1)
    chain(2)
    for copy in backs:
        copy.wait_recv()
    outer_forward(2)
    chain(5)
    for k in range(3):
        chain(1)
        outer_finish(k)
    chain(CHUNKS + LAG)

    @pl.when(is_mid)
    def _():
        def step(k, _):
            mid_copy(k).wait_send()
            total_copy(k).wait_send()
            return 0

        lax.fori_loop(0, CHUNKS, step, 0)
        for k in range(5):
            hidden_copy(seq, k, beside).wait_send()

    @pl.when(is_end)
    def _():
        def step(k, _):
            end_copy(k).wait_send()
            total_copy(k).wait_recv()
            return 0

        lax.fori_loop(0, CHUNKS, step, 0)
        hidden_copy(seq, 0, beside).wait_send()
        for source in (near_end, mid, far_end):
            hidden_copy(source, 0, beside).wait_recv()

    for copy in outer_s:
        copy.wait_recv()
    own_rows.wait()
    for pair in swaps:
        for copy in pair:
            copy.wait_send()
    for copy in nears + fars + backs + outer_b + outer_f + outer_s:
        copy.wait_send()


def reduce(sums, parts, hidden, everything, outer_y, outer_x):
    vmem = pl.BlockSpec(memory_space=pltpu.VMEM)
    dma = pltpu.SemaphoreType.DMA
    slot = (SLOTS, 128, 128)
    return pl.pallas_call(
        reduce_kernel,
        out_shape=(
            jax.ShapeDtypeStruct((2, 2, 8, 16, 128), BF16),
            jax.ShapeDtypeStruct(slot, BF16),
            jax.ShapeDtypeStruct((4, COLS, 128, 128), BF16),
            jax.ShapeDtypeStruct((4, 4, 2, 8, 2, 4, 16, 128), BF16),
        ),
        in_specs=[vmem] * 6,
        out_specs=(vmem,) * 4,
        scratch_shapes=[
            pltpu.VMEM((4, 8, 2, 4, 16, 128), BF16),
            pltpu.VMEM((4, 4, 8, 2, 16, 128), BF16),
            pltpu.VMEM((4, 8, 2, 4, 16, 128), BF16),
            pltpu.VMEM((4, 4, 8, 2, 16, 128), BF16),
            pltpu.VMEM((4, 8, 2, 4, 16, 128), BF16),
            pltpu.VMEM((4, 4, 8, 2, 16, 128), BF16),
            pltpu.VMEM((8, 2, 4, 16, 128), BF16),
            pltpu.VMEM((4, 8, 2, 16, 128), BF16),
            pltpu.VMEM((4, 8, 2, 16, 128), BF16),
            pltpu.VMEM((4, 8, 2, 16, 128), BF16),
            pltpu.VMEM((2, 2, 128, 128), F32),
            pltpu.VMEM((2, 2, 8, 16, 128), BF16),
            pltpu.VMEM(slot, BF16),
            pltpu.VMEM(slot, BF16),
            pltpu.VMEM(slot, BF16),
            dma((2, 4)), dma((2, 4)), dma((2, 4)), dma((2, 4)), dma((2, 4)), dma((2, 4)),
            dma((15,)), dma((15,)),
            dma((CHUNKS,)), dma((CHUNKS,)), dma((CHUNKS,)), dma((CHUNKS,)),
            dma((CHUNKS,)), dma((CHUNKS,)),
            dma((5,)), dma((4,)), dma, dma((3, 2, 2)), dma((3, 2, 2)),
            dma((3, 2, 2)), dma((3, 2, 2)), dma((3, 2, 4)), dma((3, 2, 4)),
        ],
        compiler_params=pltpu.CompilerParams(
            collective_id=2, has_side_effects=True, vmem_limit_bytes=22 << 20
        ),
        cost_estimate=pl.CostEstimate(flops=0, bytes_accessed=64 << 20, transcendentals=0),
        name="reduce_sums",
    )(sums, parts, hidden, everything, outer_y, outer_x)


STEP = 6


def finish_kernel(
    row_hbm, col_hbm, count_ref, act_ref, gain_ref, grad_ref, sums_ref,
    hidden_ref, grads_ref, total_ref, layer_ref, gin_ref, in_ref, out_ref,
    turned, row_ref, col_ref, local_sem,
):
    first_col = lax.axis_index("hid") * COLS

    @pl.when(pl.program_id(0) == 0)
    def _():
        loads = [
            pltpu.make_async_copy(src, dst, local_sem.at[k])
            for k, (src, dst) in enumerate(
                ((row_hbm, row_ref), (col_hbm, col_ref))
            )
        ]
        for load in loads:
            load.start()
        for load in loads:
            load.wait()
        for c in range(COLS):
            for g in range(4):
                turned[c, :, g * 128 : (g + 1) * 128] = hidden_ref[g, c].T

    count = count_ref[0]
    for k in range(STEP):
        s = pl.program_id(0) * STEP + k
        row = row_ref[s]
        col = col_ref[s] - first_col
        rows = jnp.concatenate([grads_ref[g, row] for g in range(4)], axis=0)
        value = dot(turned[col], rows, ((1,), (0,)))
        out_ref[k] = jnp.where(s < count, value, 0.0)
        in_ref[k] = total_ref[s].astype(F32)

    @pl.when(pl.program_id(0) == 0)
    def _():
        sums = []
        for a in range(2):
            both = sums_ref[0, a].astype(F32) + sums_ref[1, a].astype(F32)
            sums.append(
                jnp.concatenate(
                    [both[p // 8, 2 * (p % 8) : 2 * (p % 8) + 2, :] for p in range(64)], axis=1
                )
            )
        x_hat, inv_std = layer_norm(act_ref)
        layer_ref[...] = (act_ref[...].astype(F32) + sums[0]).astype(BF16)
        scaled = sums[1] * gain_ref[...]
        mean_g = jnp.sum(scaled, axis=-1, keepdims=True) * (1.0 / WIDTH)
        mean_gx = jnp.sum(scaled * x_hat, axis=-1, keepdims=True) * (1.0 / WIDTH)
        gin_ref[...] = (
            inv_std * (scaled - mean_g - x_hat * mean_gx) + grad_ref[...].astype(F32)
        ).astype(BF16)


def finish(rows, cols, count, act, gain, grad, sums, hidden, grads, totals):
    vmem = pl.BlockSpec(memory_space=pltpu.VMEM)
    hbm = pl.BlockSpec(memory_space=pltpu.HBM)
    pin = functools.partial(pltpu.with_memory_space_constraint, memory_space=pltpu.HBM)
    block = pl.BlockSpec((STEP, 128, 128), lambda i: (i, 0, 0))
    line = pl.BlockSpec((2, WIDTH), lambda i: (0, 0))
    shape = jax.ShapeDtypeStruct((SLOTS, 128, 128), F32)
    narrow = jax.ShapeDtypeStruct((2, WIDTH), BF16)
    return pl.pallas_call(
        finish_kernel,
        grid=(SLOTS // STEP,),
        out_shape=(narrow, narrow, shape, shape),
        in_specs=[hbm] * 2 + [pl.BlockSpec(memory_space=pltpu.SMEM)] + [vmem] * 7,
        out_specs=(line, line, block, block),
        scratch_shapes=[
            pltpu.VMEM((COLS, 128, 512), BF16),
            pltpu.SMEM((SLOTS,), jnp.int32),
            pltpu.SMEM((SLOTS,), jnp.int32),
            pltpu.SemaphoreType.DMA((2,)),
        ],
        compiler_params=pltpu.CompilerParams(vmem_limit_bytes=8 << 20),
        name="block_gradients",
    )(pin(rows), pin(cols), count, act, gain, grad, sums, hidden, grads, totals)


def local(activations, ln_gain, in_blocks, out_blocks, block_row, block_col, block_count, grad_out):
    gain = ln_gain.reshape(1, WIDTH)
    everything, outer_y, outer_x = gather(activations, gain, grad_out)
    sums, parts, hidden = compute(
        block_row, block_col, block_count, everything.reshape(2, 64, 128, 128), in_blocks, out_blocks
    )
    row_sums, totals, hiddens, grads = reduce(
        sums.reshape(2, 4, 2, 8, 2, 4, 16, 128), parts, hidden, everything, outer_y, outer_x
    )
    return finish(
        block_row, block_col, block_count, activations, gain, grad_out, row_sums,
        hiddens, grads.reshape(4, 64, 128, 128), totals,
    )


def solution(mesh):
    rows, blocks, slots = P(("seq", "hid"), None), P("hid", None, None), P("hid")
    in_specs = (rows, P(), blocks, blocks, slots, slots, slots, rows)
    out_specs = (rows, rows, blocks, blocks)
    return jax.shard_map(local, mesh=mesh, in_specs=in_specs, out_specs=out_specs, check_vma=False)
```

time: 131 us -> 103 us (0.79)
  Pallas kernels: 121 us -> 102 us
  local copies, waits for them, and re-layouts: 5.47 us -> 0.02 us
  other arithmetic: 2.79 us -> 0 us
    pallas_call x2 -> x3, Pallas kernels: 114 us -> 94.1 us  [the longest x1 51.8 us: reduce(): pl.pallas_call(reduce_kernel, out_shape=(jax.ShapeDtypeStruct((2, 2, 8, 1...]
    unnamed x24 -> x6, local copies, waits for them, and re-layouts: 5.47 us -> 0.02 us
    convert_element_type x1 -> x0, other arithmetic: 2.79 us -> none  [local(): totals[SLOTS:].astype(F32)]
where the time goes in v2:
time: 103 us
  Pallas kernels  102 us (99%)
  between operations  1.35 us (1%)
    pallas_call x1, Pallas kernels, reduce(): pl.pallas_call(reduce_kernel, out_shape=(jax.ShapeDtypeStruct((2, 2, 8, 1...  51.8 us
    pallas_call x1, Pallas kernels, gather(): pl.pallas_call(gather_kernel, out_shape=(jax.ShapeDtypeStruct((2, 4, 2, 8...  36.8 us
    pallas_call x1, Pallas kernels, compute(): pl.pallas_call(compute_kernel, out_shape=(jax.ShapeDtypeStruct((2, 64, 12...  7.58 us
    pallas_call x1, Pallas kernels, finish(): pl.pallas_call(finish_kernel, grid=(SLOTS // STEP,), out_shape=(narrow, n...  5.55 us

profile of v2, /device:TPU:1, one launch (start us, length us, event | category | flops | bytes accessed | tf_op | source)
XLA Modules:
  0.0 103.0 jit_solution(12763417485082279504)
XLA Ops:
  1.3 36.8 %gather_rows.1 = (bf16[2,4,2,8,2,4,16,128]{7,6,5,4,3,2,1,0:T(8,128)(2,1)S(1)}, bf16[4,8,4,16,128]{4,3,2,1,0:T(8,128)(2,1)S(1)}, bf16[4,4,8,16,128]{4,3,2,1,0:T(8,128)(2,1)S(1)}) custom-call(bf16[2,8192]{1,0:T(2,128)(2,1)} %act_ref.1, f32[1,8192]{1,0:T(1,128)} %bitcast.7, bf16[2,8192]{1,0:T(2,128)(2,1)} %grad_ref.1), custom_call_target="tpu_custom_call" | custom-call | bytes 67108864 | tf_op jit(solution)/shard_map/gather_rows/pallas_call | solution.py:236
  38.1 7.6 %block_products.1 = (bf16[2,64,128,128]{3,2,1,0:T(8,128)(2,1)S(1)}, bf16[36,128,128]{2,1,0:T(8,128)(2,1)S(1)}, bf16[3,128,128]{2,1,0:T(8,128)(2,1)S(1)}) custom-call(s32[36]{0:T(128)} %row_hbm.3, s32[36]{0:T(128)} %col_hbm.3, s32[1]{0:T(128)S(6)} %copy.12.count_ref, bf16[2,64,128,128]{3,2,1,0:T(8,128)(2,1)S(1)} %bitcast.4, bf16[36,128,128]{2,1,0:T(8,128)(2,1)} %in_hbm.1, ...), custom_call_target="tpu_custom_call" | custom-call | tf_op jit(solution)/shard_map/block_products/pallas_call | solution.py:352
  45.6 0.0 copy-start
  45.7 0.0 copy-start.1
  45.7 0.0 copy-start.2
  45.7 51.8 %reduce_sums.1 = (bf16[2,2,8,16,128]{4,3,2,1,0:T(8,128)(2,1)S(1)}, bf16[36,128,128]{2,1,0:T(8,128)(2,1)S(1)}, bf16[4,3,128,128]{3,2,1,0:T(8,128)(2,1)S(1)}, bf16[4,4,2,8,2,4,16,128]{7,6,5,4,3,2,1,0:T(8,128)(2,1)S(1)}) custom-call(bf16[2,4,2,8,2,4,16,128]{7,6,5,4,3,2,1,0:T(8,128)(2,1)S(1)} %bitcast.6, bf16[36,128,128]{2,1,0:T(8,128)(2,1)S(1)} %get-tuple-element.16.part_ref, ...), custom_call_target="tpu_custom_call" | custom-call | bytes 67108864 | tf_op jit(solution)/shard_map/reduce_sums/pallas_call | solution.py:714
  97.5 0.0 copy-done
  97.5 0.0 copy-done.1
  97.5 0.0 copy-done.2
  97.5 5.6 %block_gradients.1 = (bf16[2,8192]{1,0:T(2,128)(2,1)}, bf16[2,8192]{1,0:T(2,128)(2,1)}, f32[36,128,128]{2,1,0:T(8,128)}, f32[36,128,128]{2,1,0:T(8,128)}) custom-call(s32[36]{0:T(128)} %row_hbm.3, s32[36]{0:T(128)} %col_hbm.3, s32[1]{0:T(128)S(6)} %copy.12.count_ref, bf16[2,8192]{1,0:T(2,128)(2,1)S(1)} %copy-done, f32[1,8192]{1,0:T(1,128)S(1)} %bitcast.8, ...), custom_call_target="tpu_custom_call" | custom-call | tf_op jit(solution)/shard_map/block_gradients/pallas_call | solution.py:819
Async XLA Ops:
  45.6 51.8 %copy-start = (bf16[2,8192]{1,0:T(2,128)(2,1)S(1)}, bf16[2,8192]{1,0:T(2,128)(2,1)}, u32[]{:S(2)}) copy-start(bf16[2,8192]{1,0:T(2,128)(2,1)} %act_ref.1) | copy-start | bytes 98308
  45.7 51.8 %copy-start.1 = (f32[8192]{0:T(1024)S(1)}, f32[8192]{0:T(1024)}, u32[]{:S(2)}) copy-start(f32[8192]{0:T(1024)} %param.9) | copy-start | bytes 98308
  45.7 51.8 %copy-start.2 = (bf16[2,8192]{1,0:T(2,128)(2,1)S(1)}, bf16[2,8192]{1,0:T(2,128)(2,1)}, u32[]{:S(2)}) copy-start(bf16[2,8192]{1,0:T(2,128)(2,1)} %grad_ref.1) | copy-start | bytes 98308

commit v3 on v2

--- a/solution.py
+++ b/solution.py
@@ -92,7 +92,8 @@
         packed[a] = wide[a].astype(BF16).reshape(8, 16, 128)
     pl.semaphore_wait(barrier, len(peers))
     near, far = [], []
-    for k, (f, px, pc) in enumerate(targets):
+    for k in [*range(7, 15), *range(7)]:
+        f, px, pc = targets[k]
         copy = remote(
             packed.at[:, px * 2 + pc], landed.at[zh, :, me], a2a_send.at[k], a2a_recv.at[k],
             peers[k],
@@ -171,14 +172,15 @@
         for a in (0, 1):
             for copy in stage_ones[f, a]:
                 copy.wait_recv()
-            block = part(f, a, x, y, None)
-            out = []
-            for d in range(2):
-                out.append(
-                    remote(block, block, s2_send.at[f, a, d], s2_recv.at[f, a, d], ahead(a, d))
-                )
-                out[-1].start()
-            stage_twos[f, a] = out
+            for n in range(2):
+                for d in range(2):
+                    half = n if d == 0 else 1 - n
+                    block = part(f, a, x, y, half)
+                    stage_twos[f, a, d, half] = remote(
+                        block, block, s2_send.at[f, a, d, half], s2_recv.at[f, a, d, half],
+                        ahead(a, d),
+                    )
+                    stage_twos[f, a, d, half].start()
         for a in (0, 1):
             swap(f, a, 0, part(f, a, x, y, None))
 
@@ -186,14 +188,16 @@
         for a in (0, 1):
             out = []
             for d in range(2):
-                stage_twos[f, a][d].wait_recv()
+                stage_twos[f, a, d, d].wait_recv()
                 block = part(f, a, xs[1 - d], ys[1 - d], d)
                 out.append(
                     remote(block, block, fw_send.at[f, a, d], fw_recv.at[f, a, d], ahead(a, d))
                 )
                 out[-1].start()
             forwards[f, a] = out
+        for a in (0, 1):
             for d in range(2):
+                stage_twos[f, a, d, 1 - d].wait_recv()
                 swap(f, a, 1 + d, part(f, a, xs[1 - d], ys[1 - d], None))
 
     def finish(f):
@@ -223,7 +227,9 @@
         copy.wait_recv()
     for copy in near + far + lines + swaps + outers:
         copy.wait_send()
-    for group in (stage_ones, stage_twos, forwards):
+    for copy in stage_twos.values():
+        copy.wait_send()
+    for group in (stage_ones, forwards):
         for copies in group.values():
             for copy in copies:
                 copy.wait_send()
@@ -250,7 +256,7 @@
             pltpu.VMEM((2, 8, 16, 128), BF16),
             pltpu.VMEM((2, 2, 8, 16, 128), BF16),
             dma((3,)), dma((15,)), dma((15,)), dma((2, 3)), dma((2, 3)),
-            dma((2, 2, 3)), dma((2, 2, 3)), dma((2, 2, 2)), dma((2, 2, 2)),
+            dma((2, 2, 3)), dma((2, 2, 3)), dma((2, 2, 2, 2)), dma((2, 2, 2, 2)),
             dma((2, 2, 2)), dma((2, 2, 2)), dma((2, 2, 4)), dma((2, 2, 4)),
             dma((2, 3, 3)), dma((2, 3, 3)),
         ],
@@ -266,12 +272,12 @@
     return lax.dot_general(a, b, (dims, ((), ())), preferred_element_type=F32)
 
 
-GROUP = 4
+GROUP = 36
 
 
 def compute_kernel(
-    row_hbm, col_hbm, count_ref, all_ref, in_hbm, out_hbm, sums_ref, grads_ref, hidden,
-    row_ref, col_ref, in_ref, out_ref, pre, grad_hidden, grad_pre, total, local_sem,
+    row_hbm, col_hbm, count_ref, all_ref, in_hbm, out_hbm, total, hidden, grad_pre,
+    row_ref, col_ref, in_ref, out_ref, pre, grad_hidden, local_sem,
 ):
     first_col = lax.axis_index("hid") * COLS
     loads = [
@@ -327,22 +333,13 @@
             h, gp = hidden[col], grad_pre[col]
             one = dot(h, out_ref[s], ((1,), (0,)))
             two = dot(gp, in_ref[s], ((1,), (1,)))
-            three = dot(all_ref[0, row], gp, ((0,), (0,)))
             parts.append((s, row, jnp.where(live, one, 0.0), jnp.where(live, two, 0.0)))
-            grads_ref[s] = jnp.where(live, three, 0.0).astype(BF16)
         for s, row, one, two in parts:
             total[0, row] += one
             total[1, row] += two
         return 0
 
     lax.fori_loop(0, SLOTS // GROUP, down, 0)
-
-    def narrow(p, _):
-        sums_ref[0, p] = total[0, p].astype(BF16)
-        sums_ref[1, p] = total[1, p].astype(BF16)
-        return 0
-
-    lax.fori_loop(0, 64, narrow, 0)
 
 
 def compute(rows, cols, count, everything, in_blocks, out_blocks):
@@ -352,8 +349,8 @@
     return pl.pallas_call(
         compute_kernel,
         out_shape=(
-            jax.ShapeDtypeStruct((2, 64, 128, 128), BF16),
-            jax.ShapeDtypeStruct((SLOTS, 128, 128), BF16),
+            jax.ShapeDtypeStruct((2, 64, 128, 128), F32),
+            jax.ShapeDtypeStruct((COLS, 128, 128), BF16),
             jax.ShapeDtypeStruct((COLS, 128, 128), BF16),
         ),
         in_specs=[hbm] * 2 + [pl.BlockSpec(memory_space=pltpu.SMEM)] + [vmem] + [hbm] * 2,
@@ -365,8 +362,6 @@
             pltpu.VMEM((SLOTS, 128, 128), BF16),
             pltpu.VMEM((COLS, 128, 128), F32),
             pltpu.VMEM((COLS, 128, 128), F32),
-            pltpu.VMEM((COLS, 128, 128), BF16),
-            pltpu.VMEM((2, 64, 128, 128), F32),
             pltpu.SemaphoreType.DMA((4,)),
         ],
         compiler_params=pltpu.CompilerParams(vmem_limit_bytes=24 << 20),
@@ -375,8 +370,8 @@
 
 
 def reduce_kernel(
-    sums_ref, part_ref, hidden_ref, all_ref, outer_y, outer_x,
-    rows, total_ref, hiddens_ref, grads_ref,
+    row_ref, col_ref, count_ref, wide_ref, hidden_ref, gp_ref, all_ref, blocks_ref, outer_y, outer_x,
+    rows, total_ref, hiddens_ref, grads_ref, sums_ref, part_ref,
     swap_a, swap_b, half_a, half_b, near_a, near_b, quart_a, quart_b, far_a, far_b,
     wide, back,
     end_in, mid_own, mid_in,
@@ -394,14 +389,47 @@
     is_end = jnp.logical_or(seq == 0, seq == 3)
     targets = [(zh, px, pc) for px, pc in octet] + [(1 - zh, px, pc) for px, pc in octet]
     targets.append((1 - zh, x, core))
-    meet(
-        [device(seq, zt, px, y, pc) for zt, px, pc in targets]
-        + [device(seq, zh, x, (y + d) % 4, core) for d in (1, 2, 3)]
-        + [device((seq + d) % 4, zh, x, y, core) for d in (1, 2, 3)]
-    )
+    peers = [device(seq, zt, px, y, pc) for zt, px, pc in targets]
+    peers += [device(seq, zh, x, (y + d) % 4, core) for d in (1, 2, 3)]
+    peers += [device((seq + d) % 4, zh, x, y, core) for d in (1, 2, 3)]
+    barrier = pltpu.get_barrier_semaphore()
+    for peer in peers:
+        pl.semaphore_signal(barrier, inc=1, device_id=peer, device_id_type=MESH)
     others = [(seq + d) % 4 for d in (1, 2, 3)]
     xs = [(x + d) % 4 for d in (1, 3, 2)]
     ys = [(y + d) % 4 for d in (1, 3, 2)]
+
+    own_rows = pltpu.make_async_copy(all_ref.at[1], grads_ref.at[seq], own_sem)
+    own_rows.start()
+
+    def narrow(v, _):
+        for c in range(2):
+            for p in range(8):
+                sums_ref[0, v, c, p] = wide_ref[0, v, c, p].astype(BF16)
+                sums_ref[1, v, c, p] = wide_ref[1, v, c, p].astype(BF16)
+        return 0
+
+    lax.fori_loop(0, 4, narrow, 0)
+    first_col = lax.axis_index("hid") * COLS
+    count = count_ref[0]
+
+    def product(g, _):
+        for k in range(12):
+            s = g * 12 + k
+            row = jnp.clip(row_ref[s], 0, 63)
+            col = jnp.clip(col_ref[s] - first_col, 0, COLS - 1)
+            value = dot(blocks_ref[0, row], gp_ref[col], ((0,), (0,)))
+            part_ref[s] = jnp.where(s < count, value, 0.0).astype(BF16)
+        return 0
+
+    lax.fori_loop(0, SLOTS // 12, product, 0)
+    hiddens_ref[seq] = hidden_ref[...]
+    for other in others:
+        for n in range(8):
+            grads_ref[other, x, core, n, zh] = outer_y[other, n]
+        for n in range(4):
+            grads_ref[other, n, core, :, 1 - zh, y] = outer_x[other, n]
+    pl.semaphore_wait(barrier, len(peers))
 
     def chunk(ref, k):
         return ref.at[pl.ds(k * CHUNK, CHUNK)]
@@ -463,9 +491,6 @@
             copy.start()
         swaps.append(pair)
 
-    own_rows = pltpu.make_async_copy(all_ref.at[1], grads_ref.at[seq], own_sem)
-    own_rows.start()
-    hiddens_ref[seq] = hidden_ref[...]
     near_end = seq + 1 - 2 * (seq % 2)
     mid = 3 - seq
     far_end = mid + 1 - 2 * (mid % 2)
@@ -476,12 +501,6 @@
 
     outer_b, outer_f, outer_s = [], [], []
     planes = (zh, 1 - zh)
-    for other in others:
-        for n in range(8):
-            grads_ref[other, x, core, n, zh] = outer_y[other, n]
-        for n in range(4):
-            grads_ref[other, n, core, :, 1 - zh, y] = outer_x[other, n]
-
     def outer_block(other, f, nx, ny, half):
         if f:
             if half is None:
@@ -546,7 +565,6 @@
         hidden_copy(seq, 0, beside).start()
         hidden_copy(seq, 1, across).start()
 
-    outer_second(0)
     nears = []
     for d, (copy_a, copy_b) in zip(order[:3], swaps):
         copy_a.wait_recv()
@@ -625,6 +643,7 @@
                    device(seq, zh, (x + d) % 4, y, core))
         )
         fars[-1].start()
+    outer_second(0)
     outer_second(1)
     outer_second(2)
     for copy in fars:
@@ -707,7 +726,7 @@
         copy.wait_send()
 
 
-def reduce(sums, parts, hidden, everything, outer_y, outer_x):
+def reduce(slot_rows, slot_cols, count, sums, hidden, grad_pre, everything, outer_y, outer_x):
     vmem = pl.BlockSpec(memory_space=pltpu.VMEM)
     dma = pltpu.SemaphoreType.DMA
     slot = (SLOTS, 128, 128)
@@ -719,9 +738,11 @@
             jax.ShapeDtypeStruct((4, COLS, 128, 128), BF16),
             jax.ShapeDtypeStruct((4, 4, 2, 8, 2, 4, 16, 128), BF16),
         ),
-        in_specs=[vmem] * 6,
+        in_specs=[pl.BlockSpec(memory_space=pltpu.SMEM)] * 3 + [vmem] * 7,
         out_specs=(vmem,) * 4,
         scratch_shapes=[
+            pltpu.VMEM((2, 4, 2, 8, 2, 4, 16, 128), BF16),
+            pltpu.VMEM(slot, BF16),
             pltpu.VMEM((4, 8, 2, 4, 16, 128), BF16),
             pltpu.VMEM((4, 4, 8, 2, 16, 128), BF16),
             pltpu.VMEM((4, 8, 2, 4, 16, 128), BF16),
@@ -745,14 +766,17 @@
             dma((3, 2, 2)), dma((3, 2, 2)), dma((3, 2, 4)), dma((3, 2, 4)),
         ],
         compiler_params=pltpu.CompilerParams(
-            collective_id=2, has_side_effects=True, vmem_limit_bytes=22 << 20
+            collective_id=2, has_side_effects=True, vmem_limit_bytes=24 << 20
         ),
         cost_estimate=pl.CostEstimate(flops=0, bytes_accessed=64 << 20, transcendentals=0),
         name="reduce_sums",
-    )(sums, parts, hidden, everything, outer_y, outer_x)
-
-
-STEP = 6
+    )(
+        slot_rows, slot_cols, count, sums, hidden, grad_pre,
+        everything, everything.reshape(2, 64, 128, 128), outer_y, outer_x,
+    )
+
+
+STEP = 36
 
 
 def finish_kernel(
@@ -836,11 +860,12 @@
 def local(activations, ln_gain, in_blocks, out_blocks, block_row, block_col, block_count, grad_out):
     gain = ln_gain.reshape(1, WIDTH)
     everything, outer_y, outer_x = gather(activations, gain, grad_out)
-    sums, parts, hidden = compute(
+    sums, hidden, grad_pre = compute(
         block_row, block_col, block_count, everything.reshape(2, 64, 128, 128), in_blocks, out_blocks
     )
     row_sums, totals, hiddens, grads = reduce(
-        sums.reshape(2, 4, 2, 8, 2, 4, 16, 128), parts, hidden, everything, outer_y, outer_x
+        block_row, block_col, block_count, sums.reshape(2, 4, 2, 8, 2, 4, 16, 128), hidden, grad_pre,
+        everything, outer_y, outer_x,
     )
     return finish(
         block_row, block_col, block_count, activations, gain, grad_out, row_sums,

time: 103 us -> 99.5 us (0.966)
  Pallas kernels: 102 us -> 97.9 us
    pallas_call x1, Pallas kernels: 7.58 us -> 4.62 us  [compute(): pl.pallas_call(compute_kernel, out_shape=(jax.ShapeDtypeStruct((2, 64, 12...]
    pallas_call x1, Pallas kernels: 5.55 us -> 4.45 us  [finish(): pl.pallas_call(finish_kernel, grid=(SLOTS // STEP,), out_shape=(narrow, n...]
where the time goes in v3:
time: 99.5 us; the launch traced here: 99.3 us
  Pallas kernels  97.9 us (98%)
  between operations  1.38 us (1%)
    pallas_call x1, Pallas kernels, reduce(): pl.pallas_call(reduce_kernel, out_shape=(jax.ShapeDtypeStruct((2, 2, 8, 1...  52.6 us
    pallas_call x1, Pallas kernels, gather(): pl.pallas_call(gather_kernel, out_shape=(jax.ShapeDtypeStruct((2, 4, 2, 8...  36.2 us
    pallas_call x1, Pallas kernels, compute(): pl.pallas_call(compute_kernel, out_shape=(jax.ShapeDtypeStruct((2, 64, 12...  4.62 us
    pallas_call x1, Pallas kernels, finish(): pl.pallas_call(finish_kernel, grid=(SLOTS // STEP,), out_shape=(narrow, n...  4.45 us

profile of v3, /device:TPU:1, one launch (start us, length us, event | category | flops | bytes accessed | tf_op | source)
XLA Modules:
  0.0 99.3 jit_solution(15603609786480222829)
XLA Ops:
  1.3 36.2 %gather_rows.1 = (bf16[2,4,2,8,2,4,16,128]{7,6,5,4,3,2,1,0:T(8,128)(2,1)S(1)}, bf16[4,8,4,16,128]{4,3,2,1,0:T(8,128)(2,1)S(1)}, bf16[4,4,8,16,128]{4,3,2,1,0:T(8,128)(2,1)S(1)}) custom-call(bf16[2,8192]{1,0:T(2,128)(2,1)} %act_ref.1, f32[1,8192]{1,0:T(1,128)} %bitcast.8, bf16[2,8192]{1,0:T(2,128)(2,1)} %grad_ref.1), custom_call_target="tpu_custom_call" | custom-call | bytes 67108864 | tf_op jit(solution)/shard_map/gather_rows/pallas_call | solution.py:242
  37.5 0.0 copy-start.3
  37.5 0.0 copy-start.4
  37.5 4.6 %block_products.1 = (f32[2,64,128,128]{3,2,1,0:T(8,128)S(1)}, bf16[3,128,128]{2,1,0:T(8,128)(2,1)S(1)}, bf16[3,128,128]{2,1,0:T(8,128)(2,1)S(1)}) custom-call(s32[36]{0:T(128)} %row_hbm.3, s32[36]{0:T(128)} %col_hbm.3, s32[1]{0:T(128)S(6)} %copy.12.count_ref, bf16[2,64,128,128]{3,2,1,0:T(8,128)(2,1)S(1)} %bitcast.4, bf16[36,128,128]{2,1,0:T(8,128)(2,1)} %in_hbm.1, ...), custom_call_target="tpu_custom_call" | custom-call | tf_op jit(solution)/shard_map/block_products/pallas_call | solution.py:349
  42.2 0.0 copy-done.3
  42.2 0.0 copy-done.4
  42.2 0.0 copy-start
  42.2 0.0 copy-start.1
  42.2 0.0 copy-start.2
  42.2 52.6 %reduce_sums.1 = (bf16[2,2,8,16,128]{4,3,2,1,0:T(8,128)(2,1)S(1)}, bf16[36,128,128]{2,1,0:T(8,128)(2,1)S(1)}, bf16[4,3,128,128]{3,2,1,0:T(8,128)(2,1)S(1)}, bf16[4,4,2,8,2,4,16,128]{7,6,5,4,3,2,1,0:T(8,128)(2,1)S(1)}) custom-call(s32[36]{0:T(128)S(1)} %copy-done.3, s32[36]{0:T(128)S(1)} %copy-done.4, s32[1]{0:T(128)S(6)} %copy.12.count_ref, ...), custom_call_target="tpu_custom_call" | custom-call | bytes 67108864 | tf_op jit(solution)/shard_map/reduce_sums/pallas_call | solution.py:733
  94.8 0.0 copy-done
  94.8 0.0 copy-done.1
  94.8 0.0 copy-done.2
  94.8 4.4 %block_gradients.1 = (bf16[2,8192]{1,0:T(2,128)(2,1)}, bf16[2,8192]{1,0:T(2,128)(2,1)}, f32[36,128,128]{2,1,0:T(8,128)}, f32[36,128,128]{2,1,0:T(8,128)}) custom-call(s32[36]{0:T(128)} %row_hbm.3, s32[36]{0:T(128)} %col_hbm.3, s32[1]{0:T(128)S(6)} %copy.12.count_ref, bf16[2,8192]{1,0:T(2,128)(2,1)S(1)} %copy-done, f32[1,8192]{1,0:T(1,128)S(1)} %bitcast.9, ...), custom_call_target="tpu_custom_call" | custom-call | tf_op jit(solution)/shard_map/block_gradients/pallas_call | solution.py:843
Async XLA Ops:
  37.5 4.7 %copy-start.3 = (s32[36]{0:T(128)S(1)}, s32[36]{0:T(128)}, u32[]{:S(2)}) copy-start(s32[36]{0:T(128)} %row_hbm.3) | copy-start | bytes 436
  37.5 4.6 %copy-start.4 = (s32[36]{0:T(128)S(1)}, s32[36]{0:T(128)}, u32[]{:S(2)}) copy-start(s32[36]{0:T(128)} %col_hbm.3) | copy-start | bytes 436
  42.2 52.6 %copy-start = (bf16[2,8192]{1,0:T(2,128)(2,1)S(1)}, bf16[2,8192]{1,0:T(2,128)(2,1)}, u32[]{:S(2)}) copy-start(bf16[2,8192]{1,0:T(2,128)(2,1)} %act_ref.1) | copy-start | bytes 98308
  42.2 52.6 %copy-start.1 = (f32[8192]{0:T(1024)S(1)}, f32[8192]{0:T(1024)}, u32[]{:S(2)}) copy-start(f32[8192]{0:T(1024)} %param.9) | copy-start | bytes 98308
  42.2 52.6 %copy-start.2 = (bf16[2,8192]{1,0:T(2,128)(2,1)S(1)}, bf16[2,8192]{1,0:T(2,128)(2,1)}, u32[]{:S(2)}) copy-start(bf16[2,8192]{1,0:T(2,128)(2,1)} %grad_ref.1) | copy-start | bytes 98308

commit v4 on v3

--- a/solution.py
+++ b/solution.py
@@ -58,7 +58,7 @@
     act_hbm, gain_hbm, grad_hbm, all_ref, outer_y, outer_x,
     act_ref, gain_ref, grad_ref, wide, packed, landed,
     local_sem, a2a_send, a2a_recv, z_send, z_recv, s1_send, s1_recv,
-    s2_send, s2_recv, fw_send, fw_recv, sw_send, sw_recv, o_send, o_recv,
+    s2_send, s2_recv, fw_send, fw_recv, sw_send, sw_recv,
 ):
     seq, zh, x, y, core = place()
     me = x * 2 + core
@@ -110,7 +110,7 @@
                 second = wide[a, pl.ds(2 * p + 1, 8, stride=16), :]
                 all_ref[a, x, core, p, zp, y] = jnp.concatenate([first, second], axis=0).astype(BF16)
 
-    stage_ones, stage_twos, forwards, swaps, lines, outers = {}, {}, {}, [], [], []
+    stage_ones, stage_twos, forwards, swaps, lines = {}, {}, {}, [], []
 
     def stage_one(f):
         zp = planes[f]
@@ -135,18 +135,6 @@
                        device((seq + d) % 4, zh, x, y, core))
             )
             lines[-1].start()
-
-    def outer_first():
-        for f in range(2):
-            for k in range(3):
-                lines[3 * f + 2 - k].wait_recv()
-                block = piece(f, (seq + k + 1) % 4, x, y)
-                for d in range(3):
-                    to = device(seq, zh, xs[d], y, core) if f else device(seq, zh, x, ys[d], core)
-                    outers.append(
-                        remote(block, block, o_send.at[f, k, d], o_recv.at[f, k, d], to)
-                    )
-                    outers[-1].start()
 
     def part(f, a, nx, ny, half):
         zp = planes[f]
@@ -220,12 +208,11 @@
     stage_two(1)
     forward(0)
     forward(1)
-    outer_first()
     finish(0)
     finish(1)
-    for copy in swaps + outers:
+    for copy in swaps + lines:
         copy.wait_recv()
-    for copy in near + far + lines + swaps + outers:
+    for copy in near + far + lines + swaps:
         copy.wait_send()
     for copy in stage_twos.values():
         copy.wait_send()
@@ -258,7 +245,6 @@
             dma((3,)), dma((15,)), dma((15,)), dma((2, 3)), dma((2, 3)),
             dma((2, 2, 3)), dma((2, 2, 3)), dma((2, 2, 2, 2)), dma((2, 2, 2, 2)),
             dma((2, 2, 2)), dma((2, 2, 2)), dma((2, 2, 4)), dma((2, 2, 4)),
-            dma((2, 3, 3)), dma((2, 3, 3)),
         ],
         compiler_params=pltpu.CompilerParams(
             collective_id=1, has_side_effects=True, vmem_limit_bytes=12 << 20
@@ -377,7 +363,7 @@
     end_in, mid_own, mid_in,
     sw_send, sw_recv, n_send, n_recv, f_send, f_recv, b_send, b_recv,
     e_send, e_recv, m_send, m_recv, t_send, t_recv,
-    h_send, h_recv, own_sem, ob_send, ob_recv, of_send, of_recv, os_send, os_recv,
+    h_send, h_recv, own_sem, oa_send, oa_recv, ob_send, ob_recv, of_send, of_recv, os_send, os_recv,
 ):
     seq, zh, x, y, core = place()
     me = x * 2 + core
@@ -426,9 +412,8 @@
     hiddens_ref[seq] = hidden_ref[...]
     for other in others:
         for n in range(8):
-            grads_ref[other, x, core, n, zh] = outer_y[other, n]
-        for n in range(4):
-            grads_ref[other, n, core, :, 1 - zh, y] = outer_x[other, n]
+            grads_ref[other, x, core, n, zh, y] = outer_y[other, n, y]
+            grads_ref[other, x, core, n, 1 - zh, y] = outer_x[other, x, n]
     pl.semaphore_wait(barrier, len(peers))
 
     def chunk(ref, k):
@@ -499,7 +484,7 @@
         block = hiddens_ref.at[source]
         return remote(block, block, h_send.at[k], h_recv.at[source], to)
 
-    outer_b, outer_f, outer_s = [], [], []
+    outer_a, outer_b, outer_f, outer_s = [], [], [], []
     planes = (zh, 1 - zh)
     def outer_block(other, f, nx, ny, half):
         if f:
@@ -518,8 +503,22 @@
         copy.start()
         outer_s.append(copy)
 
+    def outer_first(k):
+        other = others[k]
+        for f in range(2):
+            block = outer_x.at[other, x] if f else outer_y.at[other, :, y]
+            place_there = grads_ref.at[other, x, core, :, planes[f], y]
+            for d in range(3):
+                to = device(seq, zh, xs[d], y, core) if f else device(seq, zh, x, ys[d], core)
+                outer_a.append(
+                    remote(block, place_there, oa_send.at[k, f, d], oa_recv.at[k, f, d], to)
+                )
+                outer_a[-1].start()
+
     def outer_second(k):
         other = others[k]
+        for copy in outer_a[6 * k : 6 * k + 6]:
+            copy.wait_recv()
         for f in range(2):
             block = outer_block(other, f, x, y, None)
             for d in range(2):
@@ -575,7 +574,7 @@
             ).astype(BF16)
             return 0
 
-        lax.fori_loop(0, 8, add_a, 0)
+        lax.fori_loop(0, 8, add_a, 0, unroll=4)
         nears.append(
             remote(half_a.at[d], near_a.at[d], n_send.at[0, d], n_recv.at[0, d],
                    device(seq, zh, (x + d) % 4, y, core))
@@ -591,17 +590,19 @@
                 ).astype(BF16)
             return 0
 
-        lax.fori_loop(0, 8, add_b, 0)
+        lax.fori_loop(0, 8, add_b, 0, unroll=2)
         nears.append(
             remote(half_b.at[d], near_b.at[d], n_send.at[1, d], n_recv.at[1, d],
                    device(seq, zh, x, (y + d) % 4, core))
         )
         nears[-1].start()
         chain(2)
+    for k in range(3):
+        outer_first(k)
     for copy in swaps[3]:
         copy.wait_recv()
-    for copy in nears:
-        chain(3)
+    for copy in nears[0::2]:
+        chain(5)
         copy.wait_recv()
 
     @pl.when(is_mid)
@@ -619,7 +620,7 @@
         quart_a[p] = value.astype(BF16)
         return 0
 
-    lax.fori_loop(0, 8, sum_a, 0)
+    lax.fori_loop(0, 8, sum_a, 0, unroll=4)
     fars = []
     for d in order[:3]:
         fars.append(
@@ -628,6 +629,10 @@
         )
         fars[-1].start()
 
+    for copy in nears[1::2]:
+        chain(1)
+        copy.wait_recv()
+
     def sum_b(p, _):
         for v in range(4):
             value = sums_ref[1, v, core, p, :, y].astype(F32) + swap_b[0, v, p].astype(F32)
@@ -636,7 +641,7 @@
             quart_b[v, p] = value.astype(BF16)
         return 0
 
-    lax.fori_loop(0, 8, sum_b, 0)
+    lax.fori_loop(0, 8, sum_b, 0, unroll=2)
     for d in order[:3]:
         fars.append(
             remote(quart_b.at[(x + d) % 4], far_b.at[d], f_send.at[1, d], f_recv.at[1, d],
@@ -662,7 +667,7 @@
                 wide[zt, a, pl.ds(2 * p + 1, 8, stride=16), :] = value[8:16]
         return 0
 
-    lax.fori_loop(0, 8, sum_far, 0)
+    lax.fori_loop(0, 8, sum_far, 0, unroll=4)
     for zt in range(2):
         for a in range(2):
             back[zt, a] = wide[zt, a].astype(BF16).reshape(8, 16, 128)
@@ -722,7 +727,7 @@
     for pair in swaps:
         for copy in pair:
             copy.wait_send()
-    for copy in nears + fars + backs + outer_b + outer_f + outer_s:
+    for copy in nears + fars + backs + outer_a + outer_b + outer_f + outer_s:
         copy.wait_send()
 
 
@@ -762,7 +767,7 @@
             dma((15,)), dma((15,)),
             dma((CHUNKS,)), dma((CHUNKS,)), dma((CHUNKS,)), dma((CHUNKS,)),
             dma((CHUNKS,)), dma((CHUNKS,)),
-            dma((5,)), dma((4,)), dma, dma((3, 2, 2)), dma((3, 2, 2)),
+            dma((5,)), dma((4,)), dma, dma((3, 2, 3)), dma((3, 2, 3)), dma((3, 2, 2)), dma((3, 2, 2)),
             dma((3, 2, 2)), dma((3, 2, 2)), dma((3, 2, 4)), dma((3, 2, 4)),
         ],
         compiler_params=pltpu.CompilerParams(

time: 99.5 us -> 95.9 us (0.964)
  Pallas kernels: 97.9 us -> 94.3 us
    pallas_call x1, Pallas kernels: 52.6 us -> 50.6 us  [reduce(): pl.pallas_call(reduce_kernel, out_shape=(jax.ShapeDtypeStruct((2, 2, 8, 1...]
    pallas_call x1, Pallas kernels: 36.2 us -> 34.7 us  [gather(): pl.pallas_call(gather_kernel, out_shape=(jax.ShapeDtypeStruct((2, 4, 2, 8...]
where the time goes in v4:
time: 95.9 us; the launch traced here: 95.7 us
  Pallas kernels  94.3 us (98%)
  between operations  1.38 us (1%)
    pallas_call x1, Pallas kernels, reduce(): pl.pallas_call(reduce_kernel, out_shape=(jax.ShapeDtypeStruct((2, 2, 8, 1...  50.6 us
    pallas_call x1, Pallas kernels, gather(): pl.pallas_call(gather_kernel, out_shape=(jax.ShapeDtypeStruct((2, 4, 2, 8...  34.7 us
    pallas_call x1, Pallas kernels, compute(): pl.pallas_call(compute_kernel, out_shape=(jax.ShapeDtypeStruct((2, 64, 12...  4.6 us
    pallas_call x1, Pallas kernels, finish(): pl.pallas_call(finish_kernel, grid=(SLOTS // STEP,), out_shape=(narrow, n...  4.45 us

profile of v4, /device:TPU:1, one launch (start us, length us, event | category | flops | bytes accessed | tf_op | source)
XLA Modules:
  0.0 95.7 jit_solution(1485217280822309305)
XLA Ops:
  1.3 34.7 %gather_rows.1 = (bf16[2,4,2,8,2,4,16,128]{7,6,5,4,3,2,1,0:T(8,128)(2,1)S(1)}, bf16[4,8,4,16,128]{4,3,2,1,0:T(8,128)(2,1)S(1)}, bf16[4,4,8,16,128]{4,3,2,1,0:T(8,128)(2,1)S(1)}) custom-call(bf16[2,8192]{1,0:T(2,128)(2,1)} %act_ref.1, f32[1,8192]{1,0:T(1,128)} %bitcast.8, bf16[2,8192]{1,0:T(2,128)(2,1)} %grad_ref.1), custom_call_target="tpu_custom_call" | custom-call | bytes 67108864 | tf_op jit(solution)/shard_map/gather_rows/pallas_call | solution.py:229
  36.0 0.0 copy-start.3
  36.0 0.0 copy-start.4
  36.0 4.6 %block_products.1 = (f32[2,64,128,128]{3,2,1,0:T(8,128)S(1)}, bf16[3,128,128]{2,1,0:T(8,128)(2,1)S(1)}, bf16[3,128,128]{2,1,0:T(8,128)(2,1)S(1)}) custom-call(s32[36]{0:T(128)} %row_hbm.3, s32[36]{0:T(128)} %col_hbm.3, s32[1]{0:T(128)S(6)} %copy.12.count_ref, bf16[2,64,128,128]{3,2,1,0:T(8,128)(2,1)S(1)} %bitcast.4, bf16[36,128,128]{2,1,0:T(8,128)(2,1)} %in_hbm.1, ...), custom_call_target="tpu_custom_call" | custom-call | tf_op jit(solution)/shard_map/block_products/pallas_call | solution.py:335
  40.6 0.0 copy-done.3
  40.6 0.0 copy-done.4
  40.6 0.0 copy-start
  40.6 0.0 copy-start.1
  40.6 0.0 copy-start.2
  40.6 50.6 %reduce_sums.1 = (bf16[2,2,8,16,128]{4,3,2,1,0:T(8,128)(2,1)S(1)}, bf16[36,128,128]{2,1,0:T(8,128)(2,1)S(1)}, bf16[4,3,128,128]{3,2,1,0:T(8,128)(2,1)S(1)}, bf16[4,4,2,8,2,4,16,128]{7,6,5,4,3,2,1,0:T(8,128)(2,1)S(1)}) custom-call(s32[36]{0:T(128)S(1)} %copy-done.3, s32[36]{0:T(128)S(1)} %copy-done.4, s32[1]{0:T(128)S(6)} %copy.12.count_ref, ...), custom_call_target="tpu_custom_call" | custom-call | bytes 67108864 | tf_op jit(solution)/shard_map/reduce_sums/pallas_call | solution.py:738
  91.2 0.0 copy-done
  91.2 0.0 copy-done.1
  91.2 0.0 copy-done.2
  91.3 4.5 %block_gradients.1 = (bf16[2,8192]{1,0:T(2,128)(2,1)}, bf16[2,8192]{1,0:T(2,128)(2,1)}, f32[36,128,128]{2,1,0:T(8,128)}, f32[36,128,128]{2,1,0:T(8,128)}) custom-call(s32[36]{0:T(128)} %row_hbm.3, s32[36]{0:T(128)} %col_hbm.3, s32[1]{0:T(128)S(6)} %copy.12.count_ref, bf16[2,8192]{1,0:T(2,128)(2,1)S(1)} %copy-done, f32[1,8192]{1,0:T(1,128)S(1)} %bitcast.9, ...), custom_call_target="tpu_custom_call" | custom-call | tf_op jit(solution)/shard_map/block_gradients/pallas_call | solution.py:848
Async XLA Ops:
  36.0 4.6 %copy-start.3 = (s32[36]{0:T(128)S(1)}, s32[36]{0:T(128)}, u32[]{:S(2)}) copy-start(s32[36]{0:T(128)} %row_hbm.3) | copy-start | bytes 436
  36.0 4.6 %copy-start.4 = (s32[36]{0:T(128)S(1)}, s32[36]{0:T(128)}, u32[]{:S(2)}) copy-start(s32[36]{0:T(128)} %col_hbm.3) | copy-start | bytes 436
  40.6 50.6 %copy-start = (bf16[2,8192]{1,0:T(2,128)(2,1)S(1)}, bf16[2,8192]{1,0:T(2,128)(2,1)}, u32[]{:S(2)}) copy-start(bf16[2,8192]{1,0:T(2,128)(2,1)} %act_ref.1) | copy-start | bytes 98308
  40.6 50.6 %copy-start.1 = (f32[8192]{0:T(1024)S(1)}, f32[8192]{0:T(1024)}, u32[]{:S(2)}) copy-start(f32[8192]{0:T(1024)} %param.9) | copy-start | bytes 98308
  40.6 50.6 %copy-start.2 = (bf16[2,8192]{1,0:T(2,128)(2,1)S(1)}, bf16[2,8192]{1,0:T(2,128)(2,1)}, u32[]{:S(2)}) copy-start(bf16[2,8192]{1,0:T(2,128)(2,1)} %grad_ref.1) | copy-start | bytes 98308

commit v5 on v4

--- a/solution.py
+++ b/solution.py
@@ -781,81 +781,87 @@
     )
 
 
-STEP = 36
+PIECE = 6
 
 
 def finish_kernel(
     row_hbm, col_hbm, count_ref, act_ref, gain_ref, grad_ref, sums_ref,
     hidden_ref, grads_ref, total_ref, layer_ref, gin_ref, in_ref, out_ref,
-    turned, row_ref, col_ref, local_sem,
+    turned, row_ref, col_ref, local_sem, wide_in, wide_out, in_sem, out_sem,
 ):
     first_col = lax.axis_index("hid") * COLS
 
-    @pl.when(pl.program_id(0) == 0)
-    def _():
-        loads = [
-            pltpu.make_async_copy(src, dst, local_sem.at[k])
-            for k, (src, dst) in enumerate(
-                ((row_hbm, row_ref), (col_hbm, col_ref))
-            )
-        ]
-        for load in loads:
-            load.start()
-        for load in loads:
-            load.wait()
-        for c in range(COLS):
-            for g in range(4):
-                turned[c, :, g * 128 : (g + 1) * 128] = hidden_ref[g, c].T
-
+    loads = [
+        pltpu.make_async_copy(src, dst, local_sem.at[k])
+        for k, (src, dst) in enumerate(((row_hbm, row_ref), (col_hbm, col_ref)))
+    ]
+    for load in loads:
+        load.start()
+    stores = []
+
+    def store(k, wide, hbm, sem):
+        part = pl.ds(k * PIECE, PIECE)
+        stores.append(pltpu.make_async_copy(wide.at[part], hbm.at[part], sem.at[k]))
+        stores[-1].start()
+
+    for s in range(SLOTS):
+        wide_in[s] = total_ref[s].astype(F32)
+        if s % PIECE == PIECE - 1:
+            store(s // PIECE, wide_in, in_ref, in_sem)
+    for c in range(COLS):
+        for g in range(4):
+            turned[c, :, g * 128 : (g + 1) * 128] = hidden_ref[g, c].T
+    for load in loads:
+        load.wait()
     count = count_ref[0]
-    for k in range(STEP):
-        s = pl.program_id(0) * STEP + k
+    for s in range(SLOTS):
         row = row_ref[s]
         col = col_ref[s] - first_col
         rows = jnp.concatenate([grads_ref[g, row] for g in range(4)], axis=0)
         value = dot(turned[col], rows, ((1,), (0,)))
-        out_ref[k] = jnp.where(s < count, value, 0.0)
-        in_ref[k] = total_ref[s].astype(F32)
-
-    @pl.when(pl.program_id(0) == 0)
-    def _():
-        sums = []
-        for a in range(2):
-            both = sums_ref[0, a].astype(F32) + sums_ref[1, a].astype(F32)
-            sums.append(
-                jnp.concatenate(
-                    [both[p // 8, 2 * (p % 8) : 2 * (p % 8) + 2, :] for p in range(64)], axis=1
-                )
+        wide_out[s] = jnp.where(s < count, value, 0.0)
+        if s % PIECE == PIECE - 1:
+            store(s // PIECE, wide_out, out_ref, out_sem)
+    sums = []
+    for a in range(2):
+        both = sums_ref[0, a].astype(F32) + sums_ref[1, a].astype(F32)
+        sums.append(
+            jnp.concatenate(
+                [both[p // 8, 2 * (p % 8) : 2 * (p % 8) + 2, :] for p in range(64)], axis=1
             )
-        x_hat, inv_std = layer_norm(act_ref)
-        layer_ref[...] = (act_ref[...].astype(F32) + sums[0]).astype(BF16)
-        scaled = sums[1] * gain_ref[...]
-        mean_g = jnp.sum(scaled, axis=-1, keepdims=True) * (1.0 / WIDTH)
-        mean_gx = jnp.sum(scaled * x_hat, axis=-1, keepdims=True) * (1.0 / WIDTH)
-        gin_ref[...] = (
-            inv_std * (scaled - mean_g - x_hat * mean_gx) + grad_ref[...].astype(F32)
-        ).astype(BF16)
+        )
+    x_hat, inv_std = layer_norm(act_ref)
+    layer_ref[...] = (act_ref[...].astype(F32) + sums[0]).astype(BF16)
+    scaled = sums[1] * gain_ref[...]
+    mean_g = jnp.sum(scaled, axis=-1, keepdims=True) * (1.0 / WIDTH)
+    mean_gx = jnp.sum(scaled * x_hat, axis=-1, keepdims=True) * (1.0 / WIDTH)
+    gin_ref[...] = (
+        inv_std * (scaled - mean_g - x_hat * mean_gx) + grad_ref[...].astype(F32)
+    ).astype(BF16)
+    for copy in stores:
+        copy.wait()
 
 
 def finish(rows, cols, count, act, gain, grad, sums, hidden, grads, totals):
     vmem = pl.BlockSpec(memory_space=pltpu.VMEM)
     hbm = pl.BlockSpec(memory_space=pltpu.HBM)
     pin = functools.partial(pltpu.with_memory_space_constraint, memory_space=pltpu.HBM)
-    block = pl.BlockSpec((STEP, 128, 128), lambda i: (i, 0, 0))
-    line = pl.BlockSpec((2, WIDTH), lambda i: (0, 0))
     shape = jax.ShapeDtypeStruct((SLOTS, 128, 128), F32)
     narrow = jax.ShapeDtypeStruct((2, WIDTH), BF16)
     return pl.pallas_call(
         finish_kernel,
-        grid=(SLOTS // STEP,),
         out_shape=(narrow, narrow, shape, shape),
         in_specs=[hbm] * 2 + [pl.BlockSpec(memory_space=pltpu.SMEM)] + [vmem] * 7,
-        out_specs=(line, line, block, block),
+        out_specs=(vmem, vmem, hbm, hbm),
         scratch_shapes=[
             pltpu.VMEM((COLS, 128, 512), BF16),
             pltpu.SMEM((SLOTS,), jnp.int32),
             pltpu.SMEM((SLOTS,), jnp.int32),
             pltpu.SemaphoreType.DMA((2,)),
+            pltpu.VMEM((SLOTS, 128, 128), F32),
+            pltpu.VMEM((SLOTS, 128, 128), F32),
+            pltpu.SemaphoreType.DMA((SLOTS // PIECE,)),
+            pltpu.SemaphoreType.DMA((SLOTS // PIECE,)),
         ],
         compiler_params=pltpu.CompilerParams(vmem_limit_bytes=8 << 20),
         name="block_gradients",

time: 95.9 us -> 95.2 us (level)
  no operation moved by 1% of the time
where the time goes in v5:
time: 95.2 us; the launch traced here: 95 us
  Pallas kernels  93.6 us (98%)
  between operations  1.38 us (1%)
    pallas_call x1, Pallas kernels, reduce(): pl.pallas_call(reduce_kernel, out_shape=(jax.ShapeDtypeStruct((2, 2, 8, 1...  50.6 us
    pallas_call x1, Pallas kernels, gather(): pl.pallas_call(gather_kernel, out_shape=(jax.ShapeDtypeStruct((2, 4, 2, 8...  34.7 us
    pallas_call x1, Pallas kernels, compute(): pl.pallas_call(compute_kernel, out_shape=(jax.ShapeDtypeStruct((2, 64, 12...  4.61 us
    pallas_call x1, Pallas kernels, finish(): pl.pallas_call(finish_kernel, out_shape=(narrow, narrow, shape, shape), i...  3.72 us

profile of v5, /device:TPU:1, one launch (start us, length us, event | category | flops | bytes accessed | tf_op | source)
XLA Modules:
  0.0 95.0 jit_solution(4912049643301850992)
XLA Ops:
  1.3 34.7 %gather_rows.1 = (bf16[2,4,2,8,2,4,16,128]{7,6,5,4,3,2,1,0:T(8,128)(2,1)S(1)}, bf16[4,8,4,16,128]{4,3,2,1,0:T(8,128)(2,1)S(1)}, bf16[4,4,8,16,128]{4,3,2,1,0:T(8,128)(2,1)S(1)}) custom-call(bf16[2,8192]{1,0:T(2,128)(2,1)} %act_ref.1, f32[1,8192]{1,0:T(1,128)} %bitcast.8, bf16[2,8192]{1,0:T(2,128)(2,1)} %grad_ref.1), custom_call_target="tpu_custom_call" | custom-call | bytes 67108864 | tf_op jit(solution)/shard_map/gather_rows/pallas_call | solution.py:229
  36.0 0.0 copy-start.3
  36.0 0.0 copy-start.4
  36.0 4.6 %block_products.1 = (f32[2,64,128,128]{3,2,1,0:T(8,128)S(1)}, bf16[3,128,128]{2,1,0:T(8,128)(2,1)S(1)}, bf16[3,128,128]{2,1,0:T(8,128)(2,1)S(1)}) custom-call(s32[36]{0:T(128)} %row_hbm.3, s32[36]{0:T(128)} %col_hbm.3, s32[1]{0:T(128)S(6)} %copy.12.count_ref, bf16[2,64,128,128]{3,2,1,0:T(8,128)(2,1)S(1)} %bitcast.4, bf16[36,128,128]{2,1,0:T(8,128)(2,1)} %in_hbm.1, ...), custom_call_target="tpu_custom_call" | custom-call | tf_op jit(solution)/shard_map/block_products/pallas_call | solution.py:335
  40.6 0.0 copy-done.3
  40.6 0.0 copy-done.4
  40.6 0.0 copy-start
  40.6 0.0 copy-start.1
  40.6 0.0 copy-start.2
  40.7 50.6 %reduce_sums.1 = (bf16[2,2,8,16,128]{4,3,2,1,0:T(8,128)(2,1)S(1)}, bf16[36,128,128]{2,1,0:T(8,128)(2,1)S(1)}, bf16[4,3,128,128]{3,2,1,0:T(8,128)(2,1)S(1)}, bf16[4,4,2,8,2,4,16,128]{7,6,5,4,3,2,1,0:T(8,128)(2,1)S(1)}) custom-call(s32[36]{0:T(128)S(1)} %copy-done.3, s32[36]{0:T(128)S(1)} %copy-done.4, s32[1]{0:T(128)S(6)} %copy.12.count_ref, ...), custom_call_target="tpu_custom_call" | custom-call | bytes 67108864 | tf_op jit(solution)/shard_map/reduce_sums/pallas_call | solution.py:738
  91.2 0.0 copy-done
  91.2 0.0 copy-done.1
  91.2 0.0 copy-done.2
  91.3 3.7 %block_gradients.1 = (bf16[2,8192]{1,0:T(2,128)(2,1)}, bf16[2,8192]{1,0:T(2,128)(2,1)}, f32[36,128,128]{2,1,0:T(8,128)}, f32[36,128,128]{2,1,0:T(8,128)}) custom-call(s32[36]{0:T(128)} %row_hbm.3, s32[36]{0:T(128)} %col_hbm.3, s32[1]{0:T(128)S(6)} %copy.12.count_ref, bf16[2,8192]{1,0:T(2,128)(2,1)S(1)} %copy-done, f32[1,8192]{1,0:T(1,128)S(1)} %bitcast.9, ...), custom_call_target="tpu_custom_call" | custom-call | tf_op jit(solution)/shard_map/block_gradients/pallas_call | solution.py:851
Async XLA Ops:
  36.0 4.6 %copy-start.3 = (s32[36]{0:T(128)S(1)}, s32[36]{0:T(128)}, u32[]{:S(2)}) copy-start(s32[36]{0:T(128)} %row_hbm.3) | copy-start | bytes 436
  36.0 4.6 %copy-start.4 = (s32[36]{0:T(128)S(1)}, s32[36]{0:T(128)}, u32[]{:S(2)}) copy-start(s32[36]{0:T(128)} %col_hbm.3) | copy-start | bytes 436
  40.6 50.6 %copy-start = (bf16[2,8192]{1,0:T(2,128)(2,1)S(1)}, bf16[2,8192]{1,0:T(2,128)(2,1)}, u32[]{:S(2)}) copy-start(bf16[2,8192]{1,0:T(2,128)(2,1)} %act_ref.1) | copy-start | bytes 98308
  40.6 50.6 %copy-start.1 = (f32[8192]{0:T(1024)S(1)}, f32[8192]{0:T(1024)}, u32[]{:S(2)}) copy-start(f32[8192]{0:T(1024)} %param.9) | copy-start | bytes 98308
  40.6 50.6 %copy-start.2 = (bf16[2,8192]{1,0:T(2,128)(2,1)S(1)}, bf16[2,8192]{1,0:T(2,128)(2,1)}, u32[]{:S(2)}) copy-start(bf16[2,8192]{1,0:T(2,128)(2,1)} %grad_ref.1) | copy-start | bytes 98308
